TPU v7x, 128 devices: a whole 4x4x4 slice. The times are simulated.
128 devices in a mesh: expert: 32 (over z, y, core), dp: 4 (over x).
Axes of the slice: x: 4, y: 4, z: 4, core: 2. Of those that a mesh axis runs over, the one named last changes fastest.
Arguments:
- tokens: bfloat16 [16384, 2048], P(('expert', 'dp')), may hold values from -6 to 6
- cotangent: bfloat16 [16384, 2048], P(('expert', 'dp')), may hold values from -6 to 6
- route_ids: int32 [16384, 8], P(('expert', 'dp')), may hold values from 0 to 31, all different within a row; in each aligned block of 128 rows (0 to 127, 128 to 255, ...) at most 48 rows name the same one
- gate_probs: bfloat16 [16384, 8], P(('expert', 'dp')), may hold values from 0.019897461 to 0.5
- expert_rank: int32 [32], replicated, may hold values from 0 to 31, each once
- gate_kernel: bfloat16 [32, 2048, 768], P('expert'), may hold values from -0.125 to 0.125
- lift_kernel: bfloat16 [32, 2048, 768], P('expert'), may hold values from -0.125 to 0.125
- down_kernel: bfloat16 [32, 768, 2048], P('expert'), may hold values from -0.21875 to 0.21875
Outputs:
- tokens_grad: bfloat16 [16384, 2048], P(('expert', 'dp'))
- probs_grad: bfloat16 [16384, 8], P(('expert', 'dp'))
- gate_change: float32 [32, 2048, 768], P('expert', 'dp')
- lift_change: float32 [32, 2048, 768], P('expert', 'dp')
- down_change: float32 [32, 768, 2048], P('expert', None, 'dp')
Inputs may be any that keep to these rules, and one draw needn't show every extreme that they name: `route_ids`: each token names 8 different experts; among the tokens of one device no expert is named more than 48 times. `expert_rank`: every expert once.
All inputs are finite; a program needn't handle non-finite values.
Results may differ from a plain program's by a relative error of at most 0.012.
Values may be sent and summed in bfloat16 or wider, within the bound.
A program may use at most 192 MiB of HBM per device.

v0:
```python
import jax
import jax.numpy as jnp
from jax import lax
from jax.sharding import PartitionSpec as P


def expert_pass(rows_x, rows_dy, rows_gate, kernel_gate, kernel_lift, kernel_down):
    gate_pre = jnp.dot(rows_x, kernel_gate, preferred_element_type=jnp.float32)
    lift_pre = jnp.dot(rows_x, kernel_lift, preferred_element_type=jnp.float32)
    sigmoid_part = jax.nn.sigmoid(gate_pre)
    activated = gate_pre * sigmoid_part
    hidden = (activated * lift_pre).astype(jnp.bfloat16)
    expert_out = jnp.dot(hidden, kernel_down, preferred_element_type=jnp.float32)
    prob_delta = jnp.sum(rows_dy.astype(jnp.float32) * expert_out, axis=-1).astype(jnp.bfloat16)
    scaled_cot = (rows_gate.astype(jnp.float32)[:, None] * rows_dy.astype(jnp.float32)).astype(
        jnp.bfloat16
    )
    contract_last = (((1,), (1,)), ((), ()))
    hidden_delta = lax.dot_general(
        scaled_cot, kernel_down, contract_last, preferred_element_type=jnp.float32
    )
    lift_delta = (hidden_delta * activated).astype(jnp.bfloat16)
    gate_delta = (
        hidden_delta * lift_pre * sigmoid_part * (1.0 + gate_pre * (1.0 - sigmoid_part))
    ).astype(jnp.bfloat16)
    input_delta = lax.dot_general(
        gate_delta, kernel_gate, contract_last, preferred_element_type=jnp.float32
    )
    input_delta = input_delta + lax.dot_general(
        lift_delta, kernel_lift, contract_last, preferred_element_type=jnp.float32
    )
    return (
        input_delta.astype(jnp.bfloat16),
        prob_delta,
        hidden,
        scaled_cot,
        gate_delta,
        lift_delta,
    )


def kernel_terms(rows_x, hidden, scaled_cot, gate_delta, lift_delta):
    contract_first = (((0,), (0,)), ((), ()))
    gate_term = lax.dot_general(
        rows_x, gate_delta, contract_first, preferred_element_type=jnp.float32
    )
    lift_term = lax.dot_general(
        rows_x, lift_delta, contract_first, preferred_element_type=jnp.float32
    )
    down_term = lax.dot_general(
        hidden, scaled_cot, contract_first, preferred_element_type=jnp.float32
    )
    return (jnp.stack([gate_term, lift_term], axis=1), down_term)


def slot_rows(array, lower, upper):
    return array[:, lower:upper].reshape(-1, array.shape[-1])


def shards(
    tokens, cotangent, route_ids, gate_probs, expert_rank, gate_kernel, lift_kernel, down_kernel
):
    expert_count = lax.axis_size("expert")
    group_count = lax.axis_size("dp")
    half_count = expert_count // 2
    token_count, pick_count = route_ids.shape
    width = tokens.shape[1]
    capacity = token_count * pick_count // (2 * expert_count)
    near_count = capacity // 2
    far_start = capacity + near_count
    slot_count = 2 * capacity
    route_count = token_count * pick_count
    flat_routes = route_ids.reshape(route_count)
    expert_ids = jnp.arange(expert_count, dtype=jnp.int32)
    rank_of = jnp.zeros((expert_count,), jnp.int32).at[expert_rank].set(expert_ids)
    is_hot = rank_of < half_count
    partner_of = expert_rank[jnp.minimum(rank_of + half_count, expert_count - 1)]
    hosted_of = jnp.where(is_hot, expert_ids, expert_rank[jnp.maximum(rank_of - half_count, 0)])
    one_hot = (flat_routes[:, None] == expert_ids[None, :]).astype(jnp.int32)
    earlier = jnp.cumsum(one_hot, axis=0) - one_hot
    slot_index = jnp.sum(earlier * one_hot, axis=1)
    route_hot = jnp.sum(one_hot * is_hot.astype(jnp.int32)[None, :], axis=1) > 0
    kept = (slot_index < capacity) | route_hot & (slot_index < slot_count)
    route_partner = jnp.sum(one_hot * partner_of[None, :], axis=1)
    destination = jnp.where(slot_index < far_start, flat_routes, route_partner)
    region_index = jnp.where(slot_index < far_start, slot_index, slot_index - near_count)
    position = jnp.where(kept, destination * far_start + region_index, expert_count * far_start)
    route_numbers = jnp.arange(route_count, dtype=jnp.int32)
    route_of_slot = (
        jnp.full((expert_count * far_start,), route_count, jnp.int32)
        .at[position]
        .set(route_numbers, mode="drop")
    )
    token_of_slot = route_of_slot // pick_count
    padded_tokens = jnp.concatenate([tokens, jnp.zeros((1, width), tokens.dtype)], axis=0)
    padded_cot = jnp.concatenate([cotangent, jnp.zeros((1, width), cotangent.dtype)], axis=0)
    padded_probs = jnp.concatenate(
        [gate_probs.reshape(route_count), jnp.zeros((1,), gate_probs.dtype)], axis=0
    )
    send_tokens = padded_tokens[token_of_slot].reshape(expert_count, far_start, width)
    send_cot = padded_cot[token_of_slot].reshape(expert_count, far_start, width)
    send_probs = padded_probs[route_of_slot].reshape(expert_count, far_start)
    recv_tokens, recv_cot, recv_probs = (
        lax.all_to_all(send_tokens, "expert", split_axis=0, concat_axis=0, tiled=True),
        lax.all_to_all(send_cot, "expert", split_axis=0, concat_axis=0, tiled=True),
        lax.all_to_all(send_probs, "expert", split_axis=0, concat_axis=0, tiled=True),
    )
    own_kernels = (gate_kernel[0], lift_kernel[0], down_kernel[0])
    group = lax.axis_index("dp")
    quarters = [
        lax.dynamic_index_in_dim(
            item.reshape(group_count, expert_count, -1), group, 0, keepdims=False
        )
        for item in own_kernels
    ]
    held = (
        lax.all_to_all(quarters[0], "expert", split_axis=0, concat_axis=0, tiled=True),
        lax.all_to_all(quarters[1], "expert", split_axis=0, concat_axis=0, tiled=True),
        lax.all_to_all(quarters[2], "expert", split_axis=0, concat_axis=0, tiled=True),
    )
    routed = [jnp.take(item, hosted_of, axis=0) for item in held]
    arrived = (
        lax.all_to_all(routed[0], "expert", split_axis=0, concat_axis=0, tiled=True),
        lax.all_to_all(routed[1], "expert", split_axis=0, concat_axis=0, tiled=True),
        lax.all_to_all(routed[2], "expert", split_axis=0, concat_axis=0, tiled=True),
    )
    rows_one = [item.reshape(1, -1) for item in arrived]
    joined = (
        lax.all_gather(rows_one[0], "dp", axis=0, tiled=True),
        lax.all_gather(rows_one[1], "dp", axis=0, tiled=True),
        lax.all_gather(rows_one[2], "dp", axis=0, tiled=True),
    )
    hosted_flat = [item.reshape(-1) for item in joined]
    hosted_kernels = [flat.reshape(kernel.shape) for flat, kernel in zip(hosted_flat, own_kernels)]
    primary_x = slot_rows(recv_tokens, 0, capacity)
    extra_x = slot_rows(recv_tokens, capacity, far_start)
    first = expert_pass(
        primary_x,
        slot_rows(recv_cot, 0, capacity),
        recv_probs[:, :capacity].reshape(-1),
        *own_kernels
    )
    second = expert_pass(
        extra_x,
        slot_rows(recv_cot, capacity, far_start),
        recv_probs[:, capacity:].reshape(-1),
        *hosted_kernels
    )
    input_rows = jnp.concatenate(
        [
            first[0].reshape(expert_count, capacity, width),
            second[0].reshape(expert_count, near_count, width),
        ],
        axis=1,
    )
    prob_rows = jnp.concatenate(
        [first[1].reshape(expert_count, capacity), second[1].reshape(expert_count, near_count)],
        axis=1,
    )
    own_terms = kernel_terms(primary_x, first[2], first[3], first[4], first[5])
    extra_terms = kernel_terms(extra_x, second[2], second[3], second[4], second[5])
    summed = (
        lax.psum_scatter(
            own_terms[0].astype(jnp.bfloat16), "dp", scatter_dimension=0, tiled=True
        ).astype(jnp.float32),
        lax.psum_scatter(
            own_terms[1].astype(jnp.bfloat16), "dp", scatter_dimension=1, tiled=True
        ).astype(jnp.float32),
        lax.psum_scatter(
            extra_terms[0].astype(jnp.bfloat16), "dp", scatter_dimension=0, tiled=True
        ).astype(jnp.float32),
        lax.psum_scatter(
            extra_terms[1].astype(jnp.bfloat16), "dp", scatter_dimension=1, tiled=True
        ).astype(jnp.float32),
    )
    keep_local = is_hot[lax.axis_index("expert")].astype(jnp.float32)
    outgoing_gl = (summed[2] * (1.0 - keep_local)).astype(jnp.bfloat16).reshape(expert_count, -1)
    outgoing_down = (summed[3] * (1.0 - keep_local)).astype(jnp.bfloat16).reshape(expert_count, -1)
    held_back = (
        lax.all_to_all(outgoing_gl, "expert", split_axis=0, concat_axis=0, tiled=True),
        lax.all_to_all(outgoing_down, "expert", split_axis=0, concat_axis=0, tiled=True),
    )
    owner_table = (hosted_of[None, :] == expert_ids[:, None]).astype(jnp.bfloat16)
    routed_back = [
        jnp.dot(owner_table, item, preferred_element_type=jnp.float32).astype(jnp.bfloat16)
        for item in held_back
    ]
    arrived_back = (
        lax.all_to_all(routed_back[0], "expert", split_axis=0, concat_axis=0, tiled=True),
        lax.all_to_all(routed_back[1], "expert", split_axis=0, concat_axis=0, tiled=True),
    )
    returned_gl = arrived_back[0].reshape(summed[2].shape).astype(jnp.float32)
    returned_down = arrived_back[1].reshape(summed[3].shape).astype(jnp.float32)
    gate_lift = summed[0] + keep_local * summed[2] + returned_gl
    down_sum = summed[1] + keep_local * summed[3] + returned_down
    back_rows, back_probs = (
        lax.all_to_all(input_rows, "expert", split_axis=0, concat_axis=0, tiled=True),
        lax.all_to_all(prob_rows, "expert", split_axis=0, concat_axis=0, tiled=True),
    )
    input_flat = jnp.concatenate(
        [back_rows.reshape(-1, width), jnp.zeros((1, width), jnp.bfloat16)], axis=0
    )
    prob_flat = jnp.concatenate([back_probs.reshape(-1), jnp.zeros((1,), jnp.bfloat16)], axis=0)
    per_route = input_flat[position].reshape(token_count, pick_count, width)
    tokens_grad = jnp.sum(per_route, axis=1, dtype=jnp.float32).astype(jnp.bfloat16)
    probs_grad = prob_flat[position].reshape(token_count, pick_count)
    gate_change = gate_lift[:, 0, :][None]
    lift_change = gate_lift[:, 1, :][None]
    down_change = down_sum[None]
    return (tokens_grad, probs_grad, gate_change, lift_change, down_change)


def solution(mesh):
    return jax.shard_map(
        shards,
        mesh=mesh,
        in_specs=(
            P(("expert", "dp"), None),
            P(("expert", "dp"), None),
            P(("expert", "dp"), None),
            P(("expert", "dp"), None),
            P(),
            P("expert", None, None),
            P("expert", None, None),
            P("expert", None, None),
        ),
        out_specs=(
            P(("expert", "dp"), None),
            P(("expert", "dp"), None),
            P("expert", "dp", None),
            P("expert", "dp", None),
            P("expert", None, "dp"),
        ),
        check_vma=False,
    )
```

profile of v0, /device:TPU:1, one launch (start us, length us, event | category | flops | bytes accessed | tf_op | source)
XLA Modules:
  0.0 643.9 jit_solution(9465490244274956409)
XLA Ops:
  16.8 9.6 %all-to-all-start.5 = ((bf16[32,2,6144]{2,1,0:T(2,128)(2,1)}), bf16[32,2,6144]{2,1,0:T(2,128)(2,1)}, u32[]{:S(2)}, u32[]{:S(2)}) async-start(bf16[32,2,6144]{2,1,0:T(2,128)(2,1)} %reshape.419), calls=%async_computation.5 | async-start | bytes 1572864 | tf_op jit(solution)/shard_map/all_to_all | solution.py:118
  30.6 6.8 %reshape_squeeze.9 = bf16[4,32,12288]{2,1,0:T(8,128)(2,1)} reshape(bf16[1,768,2048]{2,1,0:T(8,128)(2,1)} %param.17) | data formatting | bytes 6291456 | tf_op jit(solution)/shard_map/reshape;squeeze | solution.py:112
  43.7 7.4 %all-to-all-start.7 = ((bf16[32,2,6144]{2,1,0:T(2,128)(2,1)}), bf16[32,2,6144]{2,1,0:T(2,128)(2,1)S(1)}, u32[]{:S(2)}, u32[]{:S(2)}) async-start(bf16[32,2,6144]{2,1,0:T(2,128)(2,1)} %reshape.411), calls=%async_computation.7 | async-start | bytes 1572864 | tf_op jit(solution)/shard_map/all_to_all | solution.py:117
  54.6 10.8 %all-to-all-done.7 = bf16[32,2,6144]{2,1,0:T(2,128)(2,1)S(1)} async-done(((bf16[32,2,6144]{2,1,0:T(2,128)(2,1)}), bf16[32,2,6144]{2,1,0:T(2,128)(2,1)S(1)}, u32[]{:S(2)}, u32[]{:S(2)}) %all-to-all-start.7) | async-done | bytes 786464 | tf_op jit(solution)/shard_map/all_to_all | solution.py:117
  98.1 21.6 %all_to_all.144 = bf16[32,2,6144]{2,1,0:T(2,128)(2,1)S(1)} all-to-all(bf16[32,2,6144]{2,1,0:T(2,128)(2,1)S(1)} %reshape.413), channel_id=1, replica_groups=mesh['expert'=32,'dp'=4] {'expert'}, dimensions={0} | all-to-all | bytes 1572864 | tf_op jit(solution)/shard_map/all_to_all | solution.py:123
  123.7 17.9 %all_to_all.145 = bf16[32,2,6144]{2,1,0:T(2,128)(2,1)S(1)} all-to-all(bf16[32,2,6144]{2,1,0:T(2,128)(2,1)S(1)} %reshape.417), channel_id=1, replica_groups=mesh['expert'=32,'dp'=4] {'expert'}, dimensions={0} | all-to-all | bytes 1572864 | tf_op jit(solution)/shard_map/all_to_all | solution.py:125
  144.8 9.0 %reduce-window.6 = s32[32,8,128]{2,1,0:T(8,128)S(1)} reduce-window(s32[32,8,128]{2,1,0:T(8,128)S(1)} %fusion.54, s32[]{:T(128)} %constant.35.clone.1), window={size=1x1x128 pad=0_0x0_0x127_0}, to_apply=%region_0.0 | reduce-window | flops 4161536 | bytes 262148 | tf_op jit(solution)/shard_map/reduce-window
  185.2 10.0 %all-to-all-done.6 = bf16[32,2,6144]{2,1,0:T(2,128)(2,1)S(1)} async-done(((bf16[32,2,6144]{2,1,0:T(2,128)(2,1)}), bf16[32,2,6144]{2,1,0:T(2,128)(2,1)S(1)}, u32[]{:S(2)}, u32[]{:S(2)}) %all-to-all-start.6) | async-done | bytes 786464 | tf_op jit(solution)/shard_map/all_to_all | solution.py:124
  206.7 32.8 %all-to-all-done.2 = bf16[32,24,2048]{2,1,0:T(8,128)(2,1)} async-done(((bf16[32,24,2048]{2,1,0:T(8,128)(2,1)}), bf16[32,24,2048]{2,1,0:T(8,128)(2,1)}, u32[]{:S(2)}, u32[]{:S(2)}) %all-to-all-start.2) | async-done | bytes 3145760 | tf_op jit(solution)/shard_map/all_to_all | solution.py:104
  239.5 6.6 %all-to-all-start.1 = ((bf16[32,24,2048]{2,1,0:T(8,128)(2,1)}), bf16[32,24,2048]{2,1,0:T(8,128)(2,1)S(1)}, u32[]{:S(2)}, u32[]{:S(2)}) async-start(bf16[32,24,2048]{2,1,0:T(8,128)(2,1)} %bitcast.160), calls=%async_computation.1 | async-start | bytes 6291456 | tf_op jit(solution)/shard_map/all_to_all | solution.py:105
  246.4 21.7 %reduce.3 = bf16[4,393216]{1,0:T(4,128)(2,1)} reduce(bf16[4,1,393216]{2,1,0:T(2,128)(2,1)} %all-gather.11.cloned.1.call-done, bf16[]{:T(256)} %constant.102), dimensions={1}, to_apply=%all-gather.2.reduce_sub_computation | reduce | bytes 6291458 | tf_op jit(solution)/shard_map/all_gather | solution.py:129
  268.0 6.7 %reshape_reshape.11 = bf16[2048,768]{1,0:T(8,128)(2,1)} reshape(bf16[4,393216]{1,0:T(4,128)(2,1)} %reduce.3) | data formatting | bytes 6291456 | tf_op jit(solution)/shard_map/reshape;reshape | solution.py:134
  274.7 22.1 %reduce.1 = bf16[4,393216]{1,0:T(4,128)(2,1)} reduce(bf16[4,1,393216]{2,1,0:T(2,128)(2,1)} %all-gather.7.cloned.1.call-done, bf16[]{:T(256)} %constant.102), dimensions={1}, to_apply=%all-gather.reduce_sub_computation | reduce | bytes 6291458 | tf_op jit(solution)/shard_map/all_gather | solution.py:131
  296.8 6.5 %reshape_reshape.9 = bf16[768,2048]{1,0:T(8,128)(2,1)} reshape(bf16[4,393216]{1,0:T(4,128)(2,1)} %reduce.1) | data formatting | bytes 6291456 | tf_op jit(solution)/shard_map/reshape;reshape | solution.py:134
  303.3 19.1 %all-gather.9.cloned.1.call-done = bf16[4,1,393216]{2,1,0:T(2,128)(2,1)} async-done(((bf16[1,1,393216]{2,1,0:T(2,128)(2,1)}), bf16[4,1,393216]{2,1,0:T(2,128)(2,1)}) %all-gather.9.cloned.1.call-update) | async-done | bytes 3145744 | tf_op jit(solution)/shard_map/all_gather | solution.py:130
  322.3 21.8 %reduce.2 = bf16[4,393216]{1,0:T(4,128)(2,1)} reduce(bf16[4,1,393216]{2,1,0:T(2,128)(2,1)} %all-gather.9.cloned.1.call-done, bf16[]{:T(256)} %constant.102), dimensions={1}, to_apply=%all-gather.1.reduce_sub_computation | reduce | bytes 6291458 | tf_op jit(solution)/shard_map/all_gather | solution.py:130
  344.1 6.6 %reshape_reshape.10 = bf16[2048,768]{1,0:T(8,128)(2,1)} reshape(bf16[4,393216]{1,0:T(4,128)(2,1)} %reduce.2) | data formatting | bytes 6291456 | tf_op jit(solution)/shard_map/reshape;reshape | solution.py:134
  416.2 7.8 %all-to-all-start.10 = ((bf16[32,1,24]{2,1,0:T(2,128)(2,1)}), bf16[32,1,24]{2,1,0:T(2,128)(2,1)S(1)}, u32[]{:S(2)}, u32[]{:S(2)}) async-start(bf16[32,1,24]{2,1,0:T(2,128)(2,1)} %copy.59), calls=%async_computation.10 | async-start | bytes 32768 | tf_op jit(solution)/shard_map/all_to_all | solution.py:198
  430.8 7.6 %all-to-all-start.9 = ((bf16[32,24,2048]{2,1,0:T(8,128)(2,1)}), bf16[32,24,2048]{2,1,0:T(8,128)(2,1)S(1)}, u32[]{:S(2)}, u32[]{:S(2)}) async-start(bf16[32,24,2048]{2,1,0:T(8,128)(2,1)} %pad_maximum_fusion.2), calls=%async_computation.9 | async-start | bytes 6291456 | tf_op jit(solution)/shard_map/all_to_all | solution.py:197
  447.4 7.6 %reduce.17 = bf16[32,12288]{1,0:T(8,128)(2,1)} reduce(bf16[32,1,12288]{2,1,0:T(2,128)(2,1)} %all_to_all.128, bf16[]{:T(256)} %broadcast.283), dimensions={1}, to_apply=%all_to_all.128.reduce_sub_computation | reduce | bytes 1572866 | tf_op jit(solution)/shard_map/all_to_all | solution.py:181
  458.3 19.1 %all-to-all-done.9 = bf16[32,24,2048]{2,1,0:T(8,128)(2,1)S(1)} async-done(((bf16[32,24,2048]{2,1,0:T(8,128)(2,1)}), bf16[32,24,2048]{2,1,0:T(8,128)(2,1)S(1)}, u32[]{:S(2)}, u32[]{:S(2)}) %all-to-all-start.9) | async-done | bytes 3145760 | tf_op jit(solution)/shard_map/all_to_all | solution.py:197
  477.4 7.1 %all-to-all-start.13 = ((bf16[32,2,6144]{2,1,0:T(2,128)(2,1)}), bf16[32,2,6144]{2,1,0:T(2,128)(2,1)}, u32[]{:S(2)}, u32[]{:S(2)}) async-start(bf16[32,2,6144]{2,1,0:T(2,128)(2,1)} %reshape.427), calls=%async_computation.17 | async-start | bytes 1572864 | tf_op jit(solution)/shard_map/all_to_all | solution.py:181
  489.0 9.6 %all_to_all.127 = bf16[32,1,24576]{2,1,0:T(2,128)(2,1)} reshape(bf16[512,2,768]{2,1,0:T(2,128)(2,1)} %copy.60) | data formatting | bytes 3145728 | tf_op jit(solution)/shard_map/all_to_all | solution.py:180
  498.6 11.9 %reduce.15 = bf16[32,24576]{1,0:T(8,128)(2,1)S(1)} reduce(bf16[32,1,24576]{2,1,0:T(2,128)(2,1)} %all_to_all.127, bf16[]{:T(256)} %broadcast.283), dimensions={1}, to_apply=%all_to_all.127.reduce_sub_computation | reduce | bytes 3145730 | tf_op jit(solution)/shard_map/all_to_all | solution.py:180
  512.5 8.0 %all-to-all-start.11 = ((bf16[32,2,12288]{2,1,0:T(2,128)(2,1)}), bf16[32,2,12288]{2,1,0:T(2,128)(2,1)S(1)}, u32[]{:S(2)}, u32[]{:S(2)}) async-start(bf16[32,2,12288]{2,1,0:T(2,128)(2,1)} %reshape.423), calls=%async_computation.13 | async-start | bytes 3145728 | tf_op jit(solution)/shard_map/all_to_all | solution.py:180
  531.4 11.2 %all-to-all-done.11 = bf16[32,2,12288]{2,1,0:T(2,128)(2,1)S(1)} async-done(((bf16[32,2,12288]{2,1,0:T(2,128)(2,1)}), bf16[32,2,12288]{2,1,0:T(2,128)(2,1)S(1)}, u32[]{:S(2)}, u32[]{:S(2)}) %all-to-all-start.11) | async-done | bytes 1572896 | tf_op jit(solution)/shard_map/all_to_all | solution.py:180
  543.7 6.3 all-to-all-start.14
  549.9 8.2 %reshape.424 = bf16[32,1,24576]{2,1,0:T(2,128)(2,1)S(1)} reshape(bf16[32,2,12288]{2,1,0:T(2,128)(2,1)} %copy-done.4) | data formatting | bytes 3145728
  566.9 7.9 %all-to-all-start.12 = ((bf16[32,2,12288]{2,1,0:T(2,128)(2,1)}), bf16[32,2,12288]{2,1,0:T(2,128)(2,1)}, u32[]{:S(2)}, u32[]{:S(2)}) async-start(bf16[32,2,12288]{2,1,0:T(2,128)(2,1)} %reshape.425), calls=%async_computation.14 | async-start | bytes 3145728 | tf_op jit(solution)/shard_map/all_to_all | solution.py:189
  575.0 6.8 %gather_fusion.6 = bf16[1024]{0:T(1024)(128)(2,1)S(1)} fusion(bf16[769]{0:T(1024)(128)(2,1)S(1)} %pad_maximum_fusion.4, s32[1024]{0:T(1024)S(1)} %broadcast_clamp_fusion), kind=kCustom, calls=%fused_computation.9 | custom fusion | bytes 8192 | tf_op jit(solution)/shard_map/gather | solution.py:206
  609.2 8.4 %reshape.426 = bf16[32,1,24576]{2,1,0:T(2,128)(2,1)S(1)} reshape(bf16[32,2,12288]{2,1,0:T(2,128)(2,1)} %all-to-all-done.12) | data formatting | bytes 3145728
  617.6 10.8 %convert_reduce_fusion = f32[32,24576]{1,0:T(8,128)} fusion(bf16[32,1,24576]{2,1,0:T(2,128)(2,1)S(1)} %reshape.426), kind=kLoop, calls=%fused_computation.49 | loop fusion | flops 786432 | bytes 4718592 | tf_op jit(solution)/shard_map/convert_element_type | solution.py:192
  (235 shorter events, 253.0 us)
Async XLA Ops:
  16.8 27.0 %all-to-all-start.5 = ((bf16[32,2,6144]{2,1,0:T(2,128)(2,1)}), bf16[32,2,6144]{2,1,0:T(2,128)(2,1)}, u32[]{:S(2)}, u32[]{:S(2)}) async-start(bf16[32,2,6144]{2,1,0:T(2,128)(2,1)} %reshape.419), calls=%async_computation.5 | async-start | bytes 1572864 | tf_op jit(solution)/shard_map/all_to_all | solution.py:118
  39.8 11.3 %copy-start.14 = (bf16[32,1,12288]{2,0,1:T(8,128)(2,1)S(1)}, bf16[32,1,12288]{2,0,1:T(8,128)(2,1)}, u32[]{:S(2)}) copy-start(bf16[32,1,12288]{2,0,1:T(8,128)(2,1)} %get-tuple-element.48) | copy-start | bytes 2359300
  42.3 11.6 %copy-start = (s32[32]{0:T(128)S(1)}, s32[32]{0:T(128)}, u32[]{:S(2)}) copy-start(s32[32]{0:T(128)} %param.14) | copy-start | bytes 388
  43.7 21.6 %all-to-all-start.7 = ((bf16[32,2,6144]{2,1,0:T(2,128)(2,1)}), bf16[32,2,6144]{2,1,0:T(2,128)(2,1)S(1)}, u32[]{:S(2)}, u32[]{:S(2)}) async-start(bf16[32,2,6144]{2,1,0:T(2,128)(2,1)} %reshape.411), calls=%async_computation.7 | async-start | bytes 1572864 | tf_op jit(solution)/shard_map/all_to_all | solution.py:117
  65.4 21.4 %all-to-all-start.3 = ((bf16[32,2,6144]{2,1,0:T(2,128)(2,1)}), bf16[32,2,6144]{2,1,0:T(2,128)(2,1)}, u32[]{:S(2)}, u32[]{:S(2)}) async-start(bf16[32,2,6144]{2,1,0:T(2,128)(2,1)} %reshape.415), calls=%async_computation.3 | async-start | bytes 1572864 | tf_op jit(solution)/shard_map/all_to_all | solution.py:119
  70.1 176.2 %all-gather.11.cloned.1.call-start = ((), (), s32[]{:S(2)}) async-start(), calls=%async_computation.25 | async-start | bytes 7864320 | tf_op jit(solution)/shard_map/all_gather | solution.py:129
  98.1 23.8 %copy-start.6 = (bf16[32,1,12288]{2,0,1:T(8,128)(2,1)S(1)}, bf16[32,1,12288]{2,0,1:T(8,128)(2,1)}, u32[]{:S(2)}) copy-start(bf16[32,1,12288]{2,0,1:T(8,128)(2,1)} %get-tuple-element.44) | copy-start | bytes 2359300
  121.8 152.9 %all-gather.7.cloned.1.call-start = ((), (), s32[]{:S(2)}) async-start(), calls=%async_computation.23 | async-start | bytes 7864320 | tf_op jit(solution)/shard_map/all_gather | solution.py:131
  123.7 20.0 %copy-start.26 = (s32[128,8]{0,1:T(8,128)S(1)}, s32[128,8]{0,1:T(8,128)}, u32[]{:S(2)}) copy-start(s32[128,8]{0,1:T(8,128)} %param.12) | copy-start | bytes 12292
  141.6 12.5 %copy-start.27 = (bf16[128,8]{0,1:T(8,128)(2,1)S(1)}, bf16[128,8]{0,1:T(8,128)(2,1)}, u32[]{:S(2)}) copy-start(bf16[128,8]{0,1:T(8,128)(2,1)} %param.13) | copy-start | bytes 6148
  159.6 21.2 %copy-start.18 = (bf16[128,2048]{1,0:T(8,128)(2,1)S(1)}, bf16[128,2048]{1,0:T(8,128)(2,1)}, u32[]{:S(2)}) copy-start(bf16[128,2048]{1,0:T(8,128)(2,1)} %param.10) | copy-start | bytes 1572868
  165.3 11.2 %all-to-all-start = ((bf16[32,1,24]{2,1,0:T(2,128)(2,1)}), bf16[32,1,24]{2,1,0:T(2,128)(2,1)S(1)}, u32[]{:S(2)}, u32[]{:S(2)}) async-start(bf16[32,1,24]{2,1,0:T(2,128)(2,1)} %all_to_all.126), calls=%async_computation | async-start | bytes 32768 | tf_op jit(solution)/shard_map/all_to_all | solution.py:106
  176.6 18.6 %all-to-all-start.6 = ((bf16[32,2,6144]{2,1,0:T(2,128)(2,1)}), bf16[32,2,6144]{2,1,0:T(2,128)(2,1)S(1)}, u32[]{:S(2)}, u32[]{:S(2)}) async-start(bf16[32,2,6144]{2,1,0:T(2,128)(2,1)} %reshape.421), calls=%async_computation.6 | async-start | bytes 1572864 | tf_op jit(solution)/shard_map/all_to_all | solution.py:124
  195.1 44.3 %all-to-all-start.2 = ((bf16[32,24,2048]{2,1,0:T(8,128)(2,1)}), bf16[32,24,2048]{2,1,0:T(8,128)(2,1)}, u32[]{:S(2)}, u32[]{:S(2)}) async-start(bf16[32,24,2048]{2,1,0:T(8,128)(2,1)} %bitcast.161), calls=%async_computation.2 | async-start | bytes 6291456 | tf_op jit(solution)/shard_map/all_to_all | solution.py:104
  200.2 122.2 %all-gather.9.cloned.1.call-start = ((), (), s32[]{:S(2)}) async-start(), calls=%async_computation.24 | async-start | bytes 7864320 | tf_op jit(solution)/shard_map/all_gather | solution.py:130
  239.5 115.3 %all-to-all-start.1 = ((bf16[32,24,2048]{2,1,0:T(8,128)(2,1)}), bf16[32,24,2048]{2,1,0:T(8,128)(2,1)S(1)}, u32[]{:S(2)}, u32[]{:S(2)}) async-start(bf16[32,24,2048]{2,1,0:T(8,128)(2,1)} %bitcast.160), calls=%async_computation.1 | async-start | bytes 6291456 | tf_op jit(solution)/shard_map/all_to_all | solution.py:105
  246.0 193.6 %reduce-scatter.11.cloned.1.call-start = ((), (), s32[]{:S(2)}) async-start(), calls=%async_computation.22 | async-start | bytes 3932160 | tf_op jit(solution)/shard_map/reduce_scatter | solution.py:172
  364.1 120.4 %reduce-scatter.7.cloned.1.call-start = ((), (), s32[]{:S(2)}) async-start(), calls=%async_computation.20 | async-start | bytes 7864320 | tf_op jit(solution)/shard_map/reduce_scatter | solution.py:169
  372.1 234.3 %reduce-scatter.9.cloned.1.call-start = ((), (), s32[]{:S(2)}) async-start(), calls=%async_computation.21 | async-start | bytes 3932160 | tf_op jit(solution)/shard_map/reduce_scatter | solution.py:166
  392.2 240.4 %reduce-scatter.5.cloned.1.call-start = ((), (), s32[]{:S(2)}) async-start(), calls=%async_computation.19 | async-start | bytes 7864320 | tf_op jit(solution)/shard_map/reduce_scatter | solution.py:163
  414.5 12.4 %copy-start.3 = (bf16[2048,768]{1,0:T(8,128)(2,1)S(1)}, bf16[2048,768]{1,0:T(8,128)(2,1)}, u32[]{:S(2)}) copy-start(bf16[2048,768]{1,0:T(8,128)(2,1)} %reshape_reshape.10) | copy-start | bytes 9437188
  414.5 12.5 %copy-start.20 = (bf16[256,768]{1,0:T(8,128)(2,1)S(1)}, bf16[256,768]{1,0:T(8,128)(2,1)}, u32[]{:S(2)}) copy-start(bf16[256,768]{1,0:T(8,128)(2,1)} %get-tuple-element.35) | copy-start | bytes 1179652
  416.2 14.6 %all-to-all-start.10 = ((bf16[32,1,24]{2,1,0:T(2,128)(2,1)}), bf16[32,1,24]{2,1,0:T(2,128)(2,1)S(1)}, u32[]{:S(2)}, u32[]{:S(2)}) async-start(bf16[32,1,24]{2,1,0:T(2,128)(2,1)} %copy.59), calls=%async_computation.10 | async-start | bytes 32768 | tf_op jit(solution)/shard_map/all_to_all | solution.py:198
  430.7 7.8 %copy-start.28 = (pred[32]{0:T(512)(128)(4,1)S(1)}, pred[32]{0:T(512)(128)(4,1)}, u32[]{:S(2)}) copy-start(pred[32]{0:T(512)(128)(4,1)} %get-tuple-element.38) | copy-start | bytes 100
  430.8 46.6 %all-to-all-start.9 = ((bf16[32,24,2048]{2,1,0:T(8,128)(2,1)}), bf16[32,24,2048]{2,1,0:T(8,128)(2,1)S(1)}, u32[]{:S(2)}, u32[]{:S(2)}) async-start(bf16[32,24,2048]{2,1,0:T(8,128)(2,1)} %pad_maximum_fusion.2), calls=%async_computation.9 | async-start | bytes 6291456 | tf_op jit(solution)/shard_map/all_to_all | solution.py:197
  477.4 11.6 %copy-start.1 = (bf16[32,24,2048]{2,1,0:T(8,128)(2,1)}, bf16[32,24,2048]{2,1,0:T(8,128)(2,1)S(1)}, u32[]{:S(2)}) copy-start(bf16[32,24,2048]{2,1,0:T(8,128)(2,1)S(1)} %all-to-all-done.9) | copy-start | bytes 9437188
  477.4 35.1 %all-to-all-start.13 = ((bf16[32,2,6144]{2,1,0:T(2,128)(2,1)}), bf16[32,2,6144]{2,1,0:T(2,128)(2,1)}, u32[]{:S(2)}, u32[]{:S(2)}) async-start(bf16[32,2,6144]{2,1,0:T(2,128)(2,1)} %reshape.427), calls=%async_computation.17 | async-start | bytes 1572864 | tf_op jit(solution)/shard_map/all_to_all | solution.py:181
  512.5 13.0 %copy-start.25 = (s32[32]{0:T(128)S(1)}, s32[32]{0:T(128)}, u32[]{:S(2)}) copy-start(s32[32]{0:T(128)} %copy-done.24) | copy-start | bytes 388
  512.5 30.1 %all-to-all-start.11 = ((bf16[32,2,12288]{2,1,0:T(2,128)(2,1)}), bf16[32,2,12288]{2,1,0:T(2,128)(2,1)S(1)}, u32[]{:S(2)}, u32[]{:S(2)}) async-start(bf16[32,2,12288]{2,1,0:T(2,128)(2,1)} %reshape.423), calls=%async_computation.13 | async-start | bytes 3145728 | tf_op jit(solution)/shard_map/all_to_all | solution.py:180
  543.7 23.2 %all-to-all-start.14 = ((bf16[32,2,6144]{2,1,0:T(2,128)(2,1)}), bf16[32,2,6144]{2,1,0:T(2,128)(2,1)}, u32[]{:S(2)}, u32[]{:S(2)}) async-start(bf16[32,2,6144]{2,1,0:T(2,128)(2,1)} %reshape.429), calls=%async_computation.18 | async-start | bytes 1572864 | tf_op jit(solution)/shard_map/all_to_all | solution.py:190
  564.8 10.0 %copy-start.22 = (s32[1024,1]{0,1:T(1,128)S(1)}, s32[1024,1]{0,1:T(1,128)}, u32[]{:S(2)}) copy-start(s32[1024,1]{0,1:T(1,128)} %get-tuple-element.24) | copy-start | bytes 12292
  566.9 42.3 %all-to-all-start.12 = ((bf16[32,2,12288]{2,1,0:T(2,128)(2,1)}), bf16[32,2,12288]{2,1,0:T(2,128)(2,1)}, u32[]{:S(2)}, u32[]{:S(2)}) async-start(bf16[32,2,12288]{2,1,0:T(2,128)(2,1)} %reshape.425), calls=%async_computation.14 | async-start | bytes 3145728 | tf_op jit(solution)/shard_map/all_to_all | solution.py:189
  (22 other events, 60.2 us)
Sparse Core Ops, SparseCore 0:
  121.9 63.1 all-gather.10
  187.3 66.3 all-gather.6
  255.9 66.3 all-gather.8
  364.2 38.9 reduce-scatter.10
  405.5 63.6 reduce-scatter.6
  471.4 37.9 reduce-scatter.8
  511.8 63.6 reduce-scatter.4
where the time goes:
time: 653 us; the launch traced here: 644 us
  local copies, waits for them, and re-layouts  185 us (28%)
  other arithmetic  154 us (24%)
  waiting for transfers between devices  108 us (17%)
  starting transfers between devices  87.6 us (13%)
  matrix products  54.2 us (8%)
  blocking collectives  39.5 us (6%)
  between operations  16 us (2%)
    unnamed x94, local copies, waits for them, and re-layouts  75.5 us
    all_to_all x1, waiting for transfers between devices, shards(): lax.all_to_all(send_tokens, 'expert', split_axis=0, concat_axis=0, tiled=...  32.8 us
    all_gather x1, other arithmetic, shards(): lax.all_gather(rows_one[2], 'dp', axis=0, tiled=True)  22.1 us
    all_gather x1, other arithmetic, shards(): lax.all_gather(rows_one[1], 'dp', axis=0, tiled=True)  21.8 us
    all_gather x1, other arithmetic, shards(): lax.all_gather(rows_one[0], 'dp', axis=0, tiled=True)  21.7 us
    all_to_all x1, blocking collectives, shards(): lax.all_to_all(routed[0], 'expert', split_axis=0, concat_axis=0, tiled=True)  21.6 us
    another operation x3, local copies, waits for them, and re-layouts, shards(): flat.reshape(kernel.shape)  19.7 us
    all_to_all x1, waiting for transfers between devices, shards(): lax.all_to_all(input_rows, 'expert', split_axis=0, concat_axis=0, tiled=T...  19.1 us
  transfers between devices with their start and end apart: 20, of which 8 were waited for; matrix products, arithmetic and copies ran while one was open for 52% of the time, Pallas kernels for 0%

commit v1 on v0

v1 whole, which is shorter than its diff:
```python
import jax
import jax.numpy as jnp
from jax import lax
from jax.sharding import PartitionSpec as P


def expert_pass(rows_x, scaled_cot, kernel_gate, kernel_lift, kernel_down):
    gate_pre = jnp.dot(rows_x, kernel_gate, preferred_element_type=jnp.float32)
    lift_pre = jnp.dot(rows_x, kernel_lift, preferred_element_type=jnp.float32)
    sigmoid_part = jax.nn.sigmoid(gate_pre)
    activated = gate_pre * sigmoid_part
    hidden = (activated * lift_pre).astype(jnp.bfloat16)
    expert_out = jnp.dot(hidden, kernel_down, preferred_element_type=jnp.float32)
    prob_delta = jnp.sum(scaled_cot.astype(jnp.float32) * expert_out, axis=-1).astype(jnp.bfloat16)
    contract_last = (((1,), (1,)), ((), ()))
    hidden_delta = lax.dot_general(
        scaled_cot, kernel_down, contract_last, preferred_element_type=jnp.float32
    )
    lift_delta = (hidden_delta * activated).astype(jnp.bfloat16)
    gate_delta = (
        hidden_delta * lift_pre * sigmoid_part * (1.0 + gate_pre * (1.0 - sigmoid_part))
    ).astype(jnp.bfloat16)
    input_delta = lax.dot_general(
        gate_delta, kernel_gate, contract_last, preferred_element_type=jnp.float32
    )
    input_delta = input_delta + lax.dot_general(
        lift_delta, kernel_lift, contract_last, preferred_element_type=jnp.float32
    )
    return (
        input_delta.astype(jnp.bfloat16),
        prob_delta,
        hidden,
        gate_delta,
        lift_delta,
    )


def kernel_terms(rows_x, hidden, scaled_cot, gate_delta, lift_delta):
    contract_first = (((0,), (0,)), ((), ()))
    gate_term = lax.dot_general(
        rows_x, gate_delta, contract_first, preferred_element_type=jnp.float32
    )
    lift_term = lax.dot_general(
        rows_x, lift_delta, contract_first, preferred_element_type=jnp.float32
    )
    down_term = lax.dot_general(
        hidden, scaled_cot, contract_first, preferred_element_type=jnp.float32
    )
    return (jnp.stack([gate_term, lift_term], axis=1), down_term)


def shards(
    tokens, cotangent, route_ids, gate_probs, expert_rank, gate_kernel, lift_kernel, down_kernel
):
    expert_count = lax.axis_size("expert")
    token_count, pick_count = route_ids.shape
    width = tokens.shape[1]
    capacity = token_count * pick_count // (2 * expert_count)
    slot_count = 2 * capacity
    expert_ids = jnp.arange(expert_count, dtype=jnp.int32)
    is_hot = jnp.any(expert_rank[: expert_count // 2, None] == expert_ids[None, :], axis=0)
    limit = jnp.where(is_hot, slot_count, capacity)
    named = route_ids[:, :, None] == expert_ids[None, None, :]
    chosen = jnp.any(named, axis=1)
    weight = jnp.sum(jnp.where(named, gate_probs.astype(jnp.float32)[:, :, None], 0.0), axis=1)
    below = jnp.tril(jnp.ones((token_count, token_count), jnp.bfloat16), -1)
    order = jnp.dot(below, chosen.astype(jnp.bfloat16), preferred_element_type=jnp.float32)
    order = order.astype(jnp.int32)
    held = chosen & (order < limit[None, :])
    pick = held[:, :, None] & (order[:, :, None] == jnp.arange(slot_count)[None, None, :])
    place = pick.astype(jnp.bfloat16).reshape(token_count, -1)
    scale = jnp.where(pick, weight[:, :, None], 0.0).astype(jnp.bfloat16)
    scale = scale.reshape(token_count, -1)
    contract_first = (((0,), (0,)), ((), ()))
    send_tokens = lax.dot_general(
        place, tokens, contract_first, preferred_element_type=jnp.float32
    ).astype(jnp.bfloat16)
    send_cot = lax.dot_general(
        scale, cotangent, contract_first, preferred_element_type=jnp.float32
    ).astype(jnp.bfloat16)
    rows_x = lax.all_to_all(send_tokens, "expert", split_axis=0, concat_axis=0, tiled=True)
    rows_sc = lax.all_to_all(send_cot, "expert", split_axis=0, concat_axis=0, tiled=True)
    own_kernels = (gate_kernel[0], lift_kernel[0], down_kernel[0])
    input_rows, prob_rows, hidden, gate_delta, lift_delta = expert_pass(
        rows_x, rows_sc, *own_kernels
    )
    gate_lift, down = kernel_terms(rows_x, hidden, rows_sc, gate_delta, lift_delta)
    gate_lift = lax.psum_scatter(
        gate_lift.astype(jnp.bfloat16), "dp", scatter_dimension=0, tiled=True
    ).astype(jnp.float32)
    down = lax.psum_scatter(
        down.astype(jnp.bfloat16), "dp", scatter_dimension=1, tiled=True
    ).astype(jnp.float32)
    back_rows = lax.all_to_all(input_rows, "expert", split_axis=0, concat_axis=0, tiled=True)
    back_probs = lax.all_to_all(
        prob_rows.reshape(expert_count, slot_count),
        "expert", split_axis=0, concat_axis=0, tiled=True,
    )
    tokens_grad = jnp.dot(place, back_rows, preferred_element_type=jnp.float32)
    by_expert = jnp.sum(
        jnp.where(pick, back_probs.astype(jnp.float32)[None], 0.0), axis=2
    )
    by_pick = jnp.sum(jnp.where(named, by_expert[:, None, :], 0.0), axis=2)
    probs_grad = (by_pick / gate_probs.astype(jnp.float32)).astype(jnp.bfloat16)
    return (
        tokens_grad.astype(jnp.bfloat16), probs_grad,
        gate_lift[:, 0][None], gate_lift[:, 1][None], down[None],
    )


def solution(mesh):
    return jax.shard_map(
        shards,
        mesh=mesh,
        in_specs=(
            P(("expert", "dp"), None),
            P(("expert", "dp"), None),
            P(("expert", "dp"), None),
            P(("expert", "dp"), None),
            P(),
            P("expert", None, None),
            P("expert", None, None),
            P("expert", None, None),
        ),
        out_specs=(
            P(("expert", "dp"), None),
            P(("expert", "dp"), None),
            P("expert", "dp", None),
            P("expert", "dp", None),
            P("expert", None, "dp"),
        ),
        check_vma=False,
    )
```

time: 653 us -> 275 us (0.42)
  local copies, waits for them, and re-layouts: 185 us -> 3.81 us
  other arithmetic: 154 us -> 11.8 us
  starting transfers between devices: 87.6 us -> 32.8 us
  blocking collectives: 39.5 us -> 0 us
  waiting for transfers between devices: 108 us -> 137 us
  matrix products: 54.2 us -> 72.9 us
    unnamed x94 -> x14, local copies, waits for them, and re-layouts: 75.5 us -> 1.18 us
    all_gather x3 -> x0, other arithmetic: 65.5 us -> none  [the longest x1 22.1 us: shards(): lax.all_gather(rows_one[2], 'dp', axis=0, tiled=True)]
    all_to_all x10 -> x1, starting transfers between devices: 67.3 us -> 6.99 us  [shards(): lax.all_to_all(prob_rows.reshape(expert_count, slot_count), 'expert', spl...]
    all_to_all x1, waiting for transfers between devices: 0.01 us -> 45.7 us  [shards(): lax.all_to_all(send_cot, 'expert', split_axis=0, concat_axis=0, tiled=True)]
    all_to_all x2 -> x0, blocking collectives: 39.5 us -> none  [the longest x1 21.6 us: shards(): lax.all_to_all(routed[0], 'expert', split_axis=0, concat_axis=0, tiled=True)]
    all_to_all x13 -> x0, other arithmetic: 37.9 us -> none  [the longest x1 11.9 us: shards(): lax.all_to_all(outgoing_gl, 'expert', split_axis=0, concat_axis=0, tiled=...]
    all_to_all x10 -> x1, waiting for transfers between devices: 36.3 us -> 0.01 us  [shards(): lax.all_to_all(prob_rows.reshape(expert_count, slot_count), 'expert', spl...]
    another operation x9 -> x1, local copies, waits for them, and re-layouts: 36.8 us -> 1.86 us  [shards(): gate_lift[:, 1][None]]
  transfers between devices with their start and end apart: 20 -> 6, of which waited for: 8 -> 3; matrix products, arithmetic and copies ran while one was open for 52% -> 20% of each run, Pallas kernels for 0% -> 0%
where the time goes in v1:
time: 275 us; the launch traced here: 272 us
  waiting for transfers between devices  137 us (50%)
  matrix products  72.9 us (27%)
  starting transfers between devices  32.8 us (12%)
  between operations  14.2 us (5%)
  other arithmetic  11.8 us (4%)
  local copies, waits for them, and re-layouts  3.81 us (1%)
    all_to_all x1, waiting for transfers between devices, shards(): lax.all_to_all(input_rows, 'expert', split_axis=0, concat_axis=0, tiled=T...  49.3 us
    all_to_all x1, waiting for transfers between devices, shards(): lax.all_to_all(send_cot, 'expert', split_axis=0, concat_axis=0, tiled=True)  45.7 us
    all_to_all x1, waiting for transfers between devices, shards(): lax.all_to_all(send_tokens, 'expert', split_axis=0, concat_axis=0, tiled=...  41.9 us
    all_to_all x1, starting transfers between devices, shards(): lax.all_to_all(send_cot, 'expert', split_axis=0, concat_axis=0, tiled=True)  9.66 us
    dot_general x1, matrix products, expert_pass(): lift_pre = jnp.dot(rows_x, kernel_lift, preferred_element_type=jnp.float32)  8.32 us
    dot_general x1, matrix products, expert_pass(): lax.dot_general(scaled_cot, kernel_down, contract_last, preferred_element...  8.23 us
    all_to_all x1, starting transfers between devices, shards(): lax.all_to_all(send_tokens, 'expert', split_axis=0, concat_axis=0, tiled=...  7.96 us
    all_to_all x1, starting transfers between devices, shards(): lax.all_to_all(input_rows, 'expert', split_axis=0, concat_axis=0, tiled=T...  7.69 us
  transfers between devices with their start and end apart: 6, of which 3 were waited for; matrix products, arithmetic and copies ran while one was open for 20% of the time, Pallas kernels for 0%

profile of v1, /device:TPU:1, one launch (start us, length us, event | category | flops | bytes accessed | tf_op | source)
XLA Modules:
  0.0 272.5 jit_solution(16251646740879529983)
XLA Ops:
  7.2 0.9 fusion.26
  8.1 0.7 convert_element_type.73
  8.8 0.7 fusion.20
  9.5 0.7 select_reduce_fusion.2
  10.8 4.2 %convolution_convert_fusion.1 = bf16[1024,2048]{1,0:T(8,128)(2,1)} fusion(bf16[128,1024]{0,1:T(8,128)(2,1)S(1)} %fusion.14, bf16[128,2048]{1,0:T(8,128)(2,1)} %param.9), kind=kOutput, calls=%fused_computation.4 | convolution fusion | flops 538968064 | bytes 4980736 | tf_op jit(solution)/shard_map/dot_general | solution.py:78
  15.0 9.7 %all-to-all-start = ((bf16[32,32,2048]{2,1,0:T(8,128)(2,1)}), bf16[32,32,2048]{2,1,0:T(8,128)(2,1)}, u32[]{:S(2)}, u32[]{:S(2)}) async-start(bf16[32,32,2048]{2,1,0:T(8,128)(2,1)} %bitcast.72), calls=%async_computation | async-start | bytes 8388608 | tf_op jit(solution)/shard_map/all_to_all | solution.py:82
  24.9 4.4 %convolution_convert_fusion = bf16[1024,2048]{1,0:T(8,128)(2,1)} fusion(pred[128,1024]{0,1:T(32,128)(4,1)S(1)} %fusion.17, bf16[128,2048]{1,0:T(8,128)(2,1)} %param.8), kind=kOutput, calls=%fused_computation.3 | convolution fusion | flops 538968064 | bytes 4849664 | tf_op jit(solution)/shard_map/dot_general | solution.py:75
  29.2 45.7 %all-to-all-done = bf16[32,32,2048]{2,1,0:T(8,128)(2,1)} async-done(((bf16[32,32,2048]{2,1,0:T(8,128)(2,1)}), bf16[32,32,2048]{2,1,0:T(8,128)(2,1)}, u32[]{:S(2)}, u32[]{:S(2)}) %all-to-all-start) | async-done | bytes 4194336 | tf_op jit(solution)/shard_map/all_to_all | solution.py:82
  74.9 8.0 %all-to-all-start.1 = ((bf16[32,32,2048]{2,1,0:T(8,128)(2,1)}), bf16[32,32,2048]{2,1,0:T(8,128)(2,1)}, u32[]{:S(2)}, u32[]{:S(2)}) async-start(bf16[32,32,2048]{2,1,0:T(8,128)(2,1)} %bitcast.71), calls=%async_computation.1 | async-start | bytes 8388608 | tf_op jit(solution)/shard_map/all_to_all | solution.py:81
  83.1 8.2 %fusion.8 = f32[1024,768]{1,0:T(8,128)} fusion(bf16[1024,2048]{1,0:T(8,128)(2,1)} %bitcast.4, bf16[1,768,2048]{2,1,0:T(8,128)(2,1)} %param.15), kind=kOutput, calls=%fused_computation.16 | convolution fusion | flops 3221225472 | bytes 10485760 | tf_op jit(solution)/shard_map/dot_general | solution.py:16
  91.4 41.9 %all-to-all-done.1 = bf16[32,32,2048]{2,1,0:T(8,128)(2,1)} async-done(((bf16[32,32,2048]{2,1,0:T(8,128)(2,1)}), bf16[32,32,2048]{2,1,0:T(8,128)(2,1)}, u32[]{:S(2)}, u32[]{:S(2)}) %all-to-all-start.1) | async-done | bytes 4194336 | tf_op jit(solution)/shard_map/all_to_all | solution.py:81
  133.3 6.3 %fusion.2 = f32[1024,768]{1,0:T(8,128)S(1)} fusion(bf16[1024,2048]{1,0:T(8,128)(2,1)} %bitcast.7, bf16[1,2048,768]{2,1,0:T(8,128)(2,1)} %param.13), kind=kOutput, calls=%fused_computation.10 | convolution fusion | flops 3221225472 | bytes 10485760 | tf_op jit(solution)/shard_map/dot_general | solution.py:8
  139.6 8.3 %multiply_convert_fusion = (bf16[1024,768]{1,0:T(8,128)(2,1)S(1)}, bf16[1024,768]{1,0:T(8,128)(2,1)}, bf16[1024,768]{1,0:T(8,128)(2,1)}) fusion(f32[1024,768]{1,0:T(8,128)S(1)} %fusion.2, f32[1024,768]{1,0:T(8,128)S(1)} %copy-done.4, bf16[1024,2048]{1,0:T(8,128)(2,1)} %bitcast.7, bf16[1,2048,768]{2,1,0:T(8,128)(2,1)S(1)} %copy-done), kind=kOutput, calls=%fused_computation.18 | convolution fusion | flops 3233021952 | bytes 18350080 | tf_op jit(solution)/shard_map/dot_general | solution.py:9
  147.9 1.1 copy-done.3
  149.0 7.1 %convolution_convert_fusion.2 = bf16[768,2048]{1,0:T(8,128)(2,1)} fusion(bf16[1024,768]{1,0:T(8,128)(2,1)S(1)} %get-tuple-element.5, bf16[1024,2048]{1,0:T(8,128)(2,1)} %bitcast.4), kind=kOutput, calls=%fused_computation.5 | convolution fusion | flops 3222798336 | bytes 8912896 | tf_op jit(solution)/shard_map/dot_general | solution.py:46
  156.1 0.3 reduce-scatter.3.cloned.1.call-start
  156.4 6.3 %fusion.11 = bf16[2048,1,768]{2,0,1:T(8,128)(2,1)S(1)} fusion(bf16[1024,2048]{1,0:T(8,128)(2,1)} %bitcast.7, bf16[1024,768]{1,0:T(8,128)(2,1)} %get-tuple-element.6), kind=kOutput, calls=%fused_computation.23 | convolution fusion | flops 3222798336 | bytes 8912896 | tf_op jit(solution)/shard_map/dot_general | solution.py:40
  162.7 5.8 %fusion.12 = bf16[2048,1,768]{2,0,1:T(8,128)(2,1)S(1)} fusion(bf16[1024,2048]{1,0:T(8,128)(2,1)} %bitcast.7, bf16[1024,768]{1,0:T(8,128)(2,1)S(1)} %copy-done.5), kind=kOutput, calls=%fused_computation.24 | convolution fusion | flops 3222798336 | bytes 8912896 | tf_op jit(solution)/shard_map/dot_general | solution.py:43
  168.6 3.2 %pad_maximum_fusion = bf16[2048,2,768]{2,0,1:T(8,128)(2,1)} fusion(bf16[2048,1,768]{2,0,1:T(8,128)(2,1)S(1)} %fusion.12, bf16[2048,1,768]{2,0,1:T(8,128)(2,1)S(1)} %fusion.11), kind=kLoop, calls=%fused_computation.2 | loop fusion | flops 3145728 | bytes 12582912 | tf_op jit(solution)/shard_map/stack | solution.py:49
  171.8 7.2 %multiply_reduce_fusion = bf16[1024]{0:T(1024)(128)(2,1)S(1)} fusion(bf16[1024,2048]{1,0:T(8,128)(2,1)} %bitcast.4, bf16[1024,768]{1,0:T(8,128)(2,1)} %copy-done.3, bf16[1,768,2048]{2,1,0:T(8,128)(2,1)} %param.15), kind=kOutput, calls=%fused_computation | convolution fusion | flops 3227515904 | bytes 8914944 | tf_op jit(solution)/shard_map/dot_general | solution.py:13
  179.0 0.7 convert_element_type.91
  179.7 7.0 %all-to-all-start.3 = ((bf16[32,1,32]{2,1,0:T(2,128)(2,1)}), bf16[32,1,32]{2,1,0:T(2,128)(2,1)S(1)}, u32[]{:S(2)}, u32[]{:S(2)}) async-start(bf16[32,1,32]{2,1,0:T(2,128)(2,1)} %convert_element_type.91), calls=%async_computation.3 | async-start | bytes 32768 | tf_op jit(solution)/shard_map/all_to_all | solution.py:95
  186.7 6.0 %fusion = f32[1024,2048]{1,0:T(8,128)S(1)} fusion(bf16[1024,768]{1,0:T(8,128)(2,1)} %get-tuple-element.6, bf16[1,2048,768]{2,1,0:T(8,128)(2,1)} %param.13), kind=kOutput, calls=%fused_computation.8 | convolution fusion | flops 3221225472 | bytes 13107200 | tf_op jit(solution)/shard_map/dot_general | solution.py:23
  192.7 5.1 %add_convert_fusion = bf16[1024,2048]{1,0:T(8,128)(2,1)} fusion(f32[1024,2048]{1,0:T(8,128)S(1)} %fusion, bf16[1024,768]{1,0:T(8,128)(2,1)S(1)} %copy-done.6, bf16[1,2048,768]{2,1,0:T(8,128)(2,1)S(1)} %copy-done), kind=kOutput, calls=%fused_computation.1 | convolution fusion | flops 3225419776 | bytes 17301504 | tf_op jit(solution)/shard_map/dot_general | solution.py:26
  197.8 7.7 %all-to-all-start.2 = ((bf16[32,32,2048]{2,1,0:T(8,128)(2,1)}), bf16[32,32,2048]{2,1,0:T(8,128)(2,1)}, u32[]{:S(2)}, u32[]{:S(2)}) async-start(bf16[32,32,2048]{2,1,0:T(8,128)(2,1)} %bitcast.73), calls=%async_computation.2 | async-start | bytes 8388608 | tf_op jit(solution)/shard_map/all_to_all | solution.py:94
  205.6 0.3 select_reduce_fusion
  205.9 0.6 divide_convert_fusion
  206.5 49.3 %all-to-all-done.2 = bf16[32,32,2048]{2,1,0:T(8,128)(2,1)} async-done(((bf16[32,32,2048]{2,1,0:T(8,128)(2,1)}), bf16[32,32,2048]{2,1,0:T(8,128)(2,1)}, u32[]{:S(2)}, u32[]{:S(2)}) %all-to-all-start.2) | async-done | bytes 4194336 | tf_op jit(solution)/shard_map/all_to_all | solution.py:94
  255.8 3.8 %fusion.13 = bf16[128,2048]{1,0:T(8,128)(2,1)} fusion(bf16[32,32,2048]{2,1,0:T(8,128)(2,1)} %all-to-all-done.2, s32[128,32]{0,1:T(8,128)S(1)} %get-tuple-element.11, pred[128,32]{0,1:T(8,128)(4,1)S(1)} %get-tuple-element.10), kind=kOutput, calls=%fused_computation.26 | convolution fusion | flops 537395200 | bytes 4739072 | tf_op jit(solution)/shard_map/dot_general | solution.py:99
  259.6 2.5 bitcast_convert_fusion
  262.1 1.6 convert_element_type.88
  263.8 1.9 slice_bitcast_fusion
  (28 shorter events, 1.1 us)
Async XLA Ops:
  7.2 132.4 %copy-start = (bf16[1,2048,768]{2,1,0:T(8,128)(2,1)S(1)}, bf16[1,2048,768]{2,1,0:T(8,128)(2,1)}, u32[]{:S(2)}) copy-start(bf16[1,2048,768]{2,1,0:T(8,128)(2,1)} %param.14) | copy-start | bytes 9437188
  15.0 59.9 %all-to-all-start = ((bf16[32,32,2048]{2,1,0:T(8,128)(2,1)}), bf16[32,32,2048]{2,1,0:T(8,128)(2,1)}, u32[]{:S(2)}, u32[]{:S(2)}) async-start(bf16[32,32,2048]{2,1,0:T(8,128)(2,1)} %bitcast.72), calls=%async_computation | async-start | bytes 8388608 | tf_op jit(solution)/shard_map/all_to_all | solution.py:82
  74.9 58.4 %all-to-all-start.1 = ((bf16[32,32,2048]{2,1,0:T(8,128)(2,1)}), bf16[32,32,2048]{2,1,0:T(8,128)(2,1)}, u32[]{:S(2)}, u32[]{:S(2)}) async-start(bf16[32,32,2048]{2,1,0:T(8,128)(2,1)} %bitcast.71), calls=%async_computation.1 | async-start | bytes 8388608 | tf_op jit(solution)/shard_map/all_to_all | solution.py:81
  82.9 176.7 %reduce-scatter.5.cloned.1.call-start = ((), (), s32[]{:S(2)}) async-start(), calls=%async_computation.7 | async-start | bytes 3932160 | tf_op jit(solution)/shard_map/reduce_scatter | solution.py:91
  133.3 6.3 %copy-start.4 = (f32[1024,768]{1,0:T(8,128)S(1)}, f32[1024,768]{1,0:T(8,128)}, u32[]{:S(2)}) copy-start(f32[1024,768]{1,0:T(8,128)} %fusion.8) | copy-start | bytes 9437188
  147.9 1.1 copy-start.3
  156.1 106.0 %reduce-scatter.3.cloned.1.call-start = ((), (), s32[]{:S(2)}) async-start(), calls=%async_computation.6 | async-start | bytes 7864320 | tf_op jit(solution)/shard_map/reduce_scatter | solution.py:88
  156.4 6.3 %copy-start.5 = (bf16[1024,768]{1,0:T(8,128)(2,1)S(1)}, bf16[1024,768]{1,0:T(8,128)(2,1)}, u32[]{:S(2)}) copy-start(bf16[1024,768]{1,0:T(8,128)(2,1)} %get-tuple-element.7) | copy-start | bytes 4718596
  179.7 18.1 %all-to-all-start.3 = ((bf16[32,1,32]{2,1,0:T(2,128)(2,1)}), bf16[32,1,32]{2,1,0:T(2,128)(2,1)S(1)}, u32[]{:S(2)}, u32[]{:S(2)}) async-start(bf16[32,1,32]{2,1,0:T(2,128)(2,1)} %convert_element_type.91), calls=%async_computation.3 | async-start | bytes 32768 | tf_op jit(solution)/shard_map/all_to_all | solution.py:95
  186.7 6.0 %copy-start.6 = (bf16[1024,768]{1,0:T(8,128)(2,1)S(1)}, bf16[1024,768]{1,0:T(8,128)(2,1)}, u32[]{:S(2)}) copy-start(bf16[1024,768]{1,0:T(8,128)(2,1)} %get-tuple-element.7) | copy-start | bytes 4718596
  197.8 8.0 %copy-start.1 = (s32[128,8]{0,1:T(8,128)S(1)}, s32[128,8]{0,1:T(8,128)}, u32[]{:S(2)}) copy-start(s32[128,8]{0,1:T(8,128)} %param.10) | copy-start | bytes 12292
  197.8 8.1 %copy-start.2 = (bf16[128,8]{0,1:T(8,128)(2,1)S(1)}, bf16[128,8]{0,1:T(8,128)(2,1)}, u32[]{:S(2)}) copy-start(bf16[128,8]{0,1:T(8,128)(2,1)} %param.11) | copy-start | bytes 6148
  197.8 58.0 %all-to-all-start.2 = ((bf16[32,32,2048]{2,1,0:T(8,128)(2,1)}), bf16[32,32,2048]{2,1,0:T(8,128)(2,1)}, u32[]{:S(2)}, u32[]{:S(2)}) async-start(bf16[32,32,2048]{2,1,0:T(8,128)(2,1)} %bitcast.73), calls=%async_computation.2 | async-start | bytes 8388608 | tf_op jit(solution)/shard_map/all_to_all | solution.py:94
Sparse Core Ops, SparseCore 0:
  156.2 37.9 reduce-scatter.4
  196.6 63.6 reduce-scatter.2

commit v2 on v1

v2 whole, which is shorter than its diff:
```python
import functools

import jax
import jax.numpy as jnp
from jax import lax
from jax.experimental import pallas as pl
from jax.experimental.pallas import tpu as pltpu
from jax.sharding import PartitionSpec as P

MESH = pl.DeviceIdType.MESH
NOTE = 128
FIRST = (((0,), (0,)), ((), ()))
LAST = (((1,), (1,)), ((), ()))
F32 = jnp.float32
BF16 = jnp.bfloat16


def dot(a, b, dims=(((1,), (0,)), ((), ()))):
    return lax.dot_general(a, b, dims, preferred_element_type=F32)


def layer_kernel(
    expert_count, group_count, slots, group_size,
    tokens, cotangent, routes, probs, rank, gate_hbm, lift_hbm, down_hbm,
    tokens_grad, probs_grad, gate_change, lift_change, down_change,
    rows_in, place, x_turned, hidden_turned, deltas, back_out, back_in, sums_gl, sums_down,
    out_sem, in_sem, back_out_sem, back_in_sem, kernel_sem,
    gl_out_sem, gl_in_sem, down_out_sem, down_in_sem,
):
    me, group = lax.axis_index("expert"), lax.axis_index("dp")
    token_count, width = tokens.shape
    pick_count = routes.shape[1]
    inner = hidden_turned.shape[0]
    row_count = expert_count * slots
    capacity = slots // 2
    quarter = width // group_count
    half_gl, half_down = quarter // 2, inner // 2
    chunk_rows = group_size * slots
    chunks = expert_count // group_size
    up, down = lax.rem(group + 1, group_count), lax.rem(group + group_count - 1, group_count)
    across = lax.rem(group + 2, group_count)

    def peer(step):
        return lax.rem(me + step, expert_count)

    barrier = pltpu.get_barrier_semaphore()

    @pl.loop(1, expert_count)
    def _(step):
        pl.semaphore_signal(barrier, inc=1, device_id=(peer(step), group), device_id_type=MESH)

    for neighbour in (up, down):
        pl.semaphore_signal(barrier, inc=1, device_id=(me, neighbour), device_id_type=MESH)

    lane = lax.broadcasted_iota(jnp.int32, (1, row_count), 1)
    lane_step = lax.shift_right_logical(lane, slots.bit_length() - 1)
    lane_expert = me + lane_step
    lane_expert = jnp.where(lane_expert >= expert_count, lane_expert - expert_count, lane_expert)
    lane_slot = lax.bitwise_and(lane, slots - 1).astype(F32)
    busy = jnp.where(rank[: expert_count // 2, :] == lane_expert, 1.0, 0.0)
    limit = capacity + (slots - capacity) * jnp.max(busy, axis=0, keepdims=True)
    gates = probs[...].astype(F32)
    chosen = jnp.zeros((token_count, row_count), F32)
    weight = jnp.zeros((token_count, row_count), F32)
    for pick in range(pick_count):
        hit = routes[:, pick : pick + 1] == lane_expert
        chosen = jnp.where(hit, 1.0, chosen)
        weight = jnp.where(hit, gates[:, pick : pick + 1], weight)
    below = jnp.where(
        lax.broadcasted_iota(jnp.int32, (token_count, token_count), 0)
        > lax.broadcasted_iota(jnp.int32, (token_count, token_count), 1),
        1.0,
        0.0,
    ).astype(BF16)
    order = dot(below, chosen.astype(BF16))
    kept = (chosen > 0.0) & (order == lane_slot) & (order < limit)
    place[...] = jnp.where(kept, 1.0, 0.0).astype(BF16)

    def first_part(rows_out, scale, gate, lift, down_kernel):
        loads = [
            pltpu.make_async_copy(source, target, kernel_sem.at[i])
            for i, (source, target) in enumerate(
                ((gate_hbm, gate), (lift_hbm, lift), (down_hbm, down_kernel))
            )
        ]
        for load in loads:
            load.start()
        scale[...] = jnp.where(kept, weight, 0.0).astype(BF16)

        def dispatch(step):
            return pltpu.make_async_remote_copy(
                src_ref=rows_out.at[step],
                dst_ref=rows_in.at[step],
                send_sem=out_sem.at[step],
                recv_sem=in_sem.at[step],
                device_id=(peer(step), group),
                device_id_type=MESH,
            )

        for part in range(chunks):
            columns = slice(part * chunk_rows, (part + 1) * chunk_rows)
            blocks = slice(part * group_size, (part + 1) * group_size)
            shape = (group_size, slots, width)
            rows_out[blocks, :slots, :] = (
                dot(place[:, columns], tokens[...], FIRST).astype(BF16).reshape(shape)
            )
            rows_out[blocks, slots:, :] = (
                dot(scale[:, columns], cotangent[...], FIRST).astype(BF16).reshape(shape)
            )
            if part == 0:
                rows_in[0] = rows_out[0]
                pl.semaphore_wait(barrier, expert_count + 1)

            @pl.loop(max(1, part * group_size), (part + 1) * group_size)
            def _(step):
                dispatch(step).start()

        for load in loads:
            load.wait()

        @pl.loop(0, chunks)
        def _(part):
            blocks = pl.ds(part * group_size, group_size)
            rows = pl.ds(pl.multiple_of(part * chunk_rows, chunk_rows), chunk_rows)

            @pl.loop(jnp.maximum(part * group_size, 1), (part + 1) * group_size)
            def _(step):
                dispatch(step).wait_recv()

            x = rows_in[blocks, :slots, :].reshape(chunk_rows, width)
            scaled = rows_in[blocks, slots:, :].reshape(chunk_rows, width)
            x_turned[:, rows] = x.T
            gate_pre = dot(x, gate[...])
            lift_pre = dot(x, lift[...])
            sigmoid = jax.nn.sigmoid(gate_pre)
            activated = gate_pre * sigmoid
            hidden = (activated * lift_pre).astype(BF16)
            hidden_turned[:, rows] = hidden.T
            expert_out = dot(hidden, down_kernel[...])
            prob = jnp.sum(scaled.astype(F32) * expert_out, axis=1, keepdims=True)
            back_out[blocks, :, width:] = (
                jnp.broadcast_to(prob, (chunk_rows, NOTE))
                .astype(BF16)
                .reshape(group_size, slots, NOTE)
            )
            hidden_delta = dot(scaled, down_kernel[...], LAST)
            lift_delta = (hidden_delta * activated).astype(BF16)
            gate_delta = (
                hidden_delta * lift_pre * sigmoid * (1.0 + gate_pre * (1.0 - sigmoid))
            ).astype(BF16)
            deltas[rows, :inner] = gate_delta
            deltas[rows, inner:] = lift_delta
            route_delta = dot(gate_delta, gate[...], LAST) + dot(lift_delta, lift[...], LAST)
            back_out[blocks, :, :width] = route_delta.astype(BF16).reshape(
                group_size, slots, width
            )

        @pl.loop(1, expert_count)
        def _(step):
            dispatch(step).wait_send()

    kernel_shape = gate_hbm.shape
    pl.run_scoped(
        first_part,
        pltpu.VMEM((expert_count, 2 * slots, width), BF16),
        pltpu.VMEM((token_count, row_count), BF16),
        pltpu.VMEM(kernel_shape, BF16),
        pltpu.VMEM(kernel_shape, BF16),
        pltpu.VMEM((inner, width), BF16),
    )

    def give_back(step):
        return pltpu.make_async_remote_copy(
            src_ref=back_out.at[step],
            dst_ref=back_in.at[step],
            send_sem=back_out_sem.at[step],
            recv_sem=back_in_sem.at[step],
            device_id=(lax.rem(me - step + expert_count, expert_count), group),
            device_id_type=MESH,
        )

    def term_gl(part, half):
        rows = pl.ds(pl.multiple_of(part * quarter + half * half_gl, half_gl), half_gl)
        return dot(x_turned[rows, :], deltas[...])

    def term_down(part, half):
        columns = pl.ds(pl.multiple_of(part * quarter, quarter), quarter)
        scaled = rows_in[:, slots:, columns].reshape(row_count, quarter)
        return dot(hidden_turned[half * half_down : (half + 1) * half_down, :], scaled)

    def second_part(partial_gl, partial_down):
        plan = (
            (across, 0, down, None),
            (across, 1, up, None),
            (up, 0, up, None),
            (down, 1, down, None),
            (down, 0, down, 0),
            (up, 1, up, 1),
        )

        def pass_on(number, kind):
            source, sink, send, receive = (
                (partial_gl, sums_gl, gl_out_sem, gl_in_sem),
                (partial_down, sums_down, down_out_sem, down_in_sem),
            )[kind]
            return pltpu.make_async_remote_copy(
                src_ref=source.at[number],
                dst_ref=sink.at[number],
                send_sem=send.at[number],
                recv_sem=receive.at[number],
                device_id=(me, plan[number][2]),
                device_id_type=MESH,
            )

        for number, (part, half, _, taken) in enumerate(plan):
            term = term_gl(part, half)
            if taken is not None:
                pass_on(taken, 0).wait_recv()
                term = term + sums_gl[taken].astype(F32)
            partial_gl[number] = term.astype(BF16)
            pass_on(number, 0).start()
            term = term_down(part, half)
            if taken is not None:
                pass_on(taken, 1).wait_recv()
                term = term + sums_down[taken].astype(F32)
            partial_down[number] = term.astype(BF16)
            pass_on(number, 1).start()
            if number == 1:

                @pl.loop(1, expert_count)
                def _(step):
                    give_back(step).start()

        for half in range(2):
            rows = slice(half * half_gl, (half + 1) * half_gl)
            term = term_gl(group, half)
            gate_change[0, rows, :] = term[:, :inner]
            lift_change[0, rows, :] = term[:, inner:]
            rows = slice(half * half_down, (half + 1) * half_down)
            down_change[0, rows, :] = term_down(group, half)

        back_in[0] = back_out[0]

        @pl.loop(1, expert_count)
        def _(step):
            give_back(step).wait_recv()

        returned = back_in[:, :, :width].reshape(row_count, width)
        tokens_grad[...] = dot(place[...], returned).astype(BF16)
        notes = back_in[:, :, width:].reshape(row_count, NOTE)
        note_row = lax.broadcasted_iota(jnp.int32, (row_count, NOTE), 0)
        note_lane = lax.broadcasted_iota(jnp.int32, (row_count, NOTE), 1)
        note_step = lax.shift_right_logical(note_row, slots.bit_length() - 1)
        notes = jnp.where(note_step == note_lane, notes.astype(F32), 0.0).astype(BF16)
        by_step = dot(place[...], notes)
        token_lane = lax.broadcasted_iota(jnp.int32, (token_count, NOTE), 1)
        pick_lane = lax.broadcasted_iota(jnp.int32, (token_count, pick_count), 1)
        total = jnp.zeros((token_count, pick_count), F32)
        for pick in range(pick_count):
            step = routes[:, pick : pick + 1] - me
            step = jnp.where(step < 0, step + expert_count, step)
            value = jnp.sum(jnp.where(token_lane == step, by_step, 0.0), axis=1, keepdims=True)
            total = jnp.where(pick_lane == pick, value, total)
        probs_grad[...] = (total / probs[...].astype(F32)).astype(BF16)

        for half, numbers in ((0, (2, 4)), (1, (3, 5))):
            rows = slice(half * half_gl, (half + 1) * half_gl)
            for number in numbers:
                pass_on(number, 0).wait_recv()
                gate_change[0, rows, :] += sums_gl[number, :, :inner].astype(F32)
                lift_change[0, rows, :] += sums_gl[number, :, inner:].astype(F32)
            rows = slice(half * half_down, (half + 1) * half_down)
            for number in numbers:
                pass_on(number, 1).wait_recv()
                down_change[0, rows, :] += sums_down[number].astype(F32)

        for number in range(len(plan)):
            for kind in range(2):
                pass_on(number, kind).wait_send()

        @pl.loop(1, expert_count)
        def _(step):
            give_back(step).wait_send()

    pl.run_scoped(
        second_part,
        pltpu.VMEM((6, half_gl, 2 * inner), BF16),
        pltpu.VMEM((6, half_down, quarter), BF16),
    )


def shards(
    tokens, cotangent, route_ids, gate_probs, expert_rank, gate_kernel, lift_kernel, down_kernel
):
    expert_count = lax.axis_size("expert")
    group_count = lax.axis_size("dp")
    token_count, pick_count = route_ids.shape
    width = tokens.shape[1]
    inner = gate_kernel.shape[2]
    slots = token_count * pick_count // expert_count
    row_count = expert_count * slots
    quarter = width // group_count
    group_size = max(1, expert_count // 4)
    flops = 2 * row_count * width * inner * 9
    vmem, anywhere = pl.BlockSpec(memory_space=pltpu.VMEM), pl.BlockSpec(memory_space=pl.ANY)
    dma = pltpu.SemaphoreType.DMA
    return pl.pallas_call(
        functools.partial(layer_kernel, expert_count, group_count, slots, group_size),
        out_shape=(
            jax.ShapeDtypeStruct(tokens.shape, BF16),
            jax.ShapeDtypeStruct(gate_probs.shape, BF16),
            jax.ShapeDtypeStruct((1, quarter, inner), F32),
            jax.ShapeDtypeStruct((1, quarter, inner), F32),
            jax.ShapeDtypeStruct((1, inner, quarter), F32),
        ),
        in_specs=[vmem] * 5 + [anywhere] * 3,
        out_specs=[vmem] * 5,
        scratch_shapes=[
            pltpu.VMEM((expert_count, 2 * slots, width), BF16),
            pltpu.VMEM((token_count, row_count), BF16),
            pltpu.VMEM((width, row_count), BF16),
            pltpu.VMEM((inner, row_count), BF16),
            pltpu.VMEM((row_count, 2 * inner), BF16),
            pltpu.VMEM((expert_count, slots, width + NOTE), BF16),
            pltpu.VMEM((expert_count, slots, width + NOTE), BF16),
            pltpu.VMEM((6, quarter // 2, 2 * inner), BF16),
            pltpu.VMEM((6, inner // 2, quarter), BF16),
            dma((expert_count,)),
            dma((expert_count,)),
            dma((expert_count,)),
            dma((expert_count,)),
            dma((3,)),
            dma((6,)),
            dma((6,)),
            dma((6,)),
            dma((6,)),
        ],
        compiler_params=pltpu.CompilerParams(
            collective_id=0, has_side_effects=True, vmem_limit_bytes=64 * 1024 * 1024
        ),
        cost_estimate=pl.CostEstimate(
            flops=flops, bytes_accessed=16 * 1024 * 1024, transcendentals=row_count * inner
        ),
    )(
        tokens,
        cotangent,
        route_ids,
        gate_probs,
        expert_rank.reshape(expert_count, 1),
        gate_kernel[0],
        lift_kernel[0],
        down_kernel[0],
    )


def solution(mesh):
    return jax.shard_map(
        shards,
        mesh=mesh,
        in_specs=(
            P(("expert", "dp"), None),
            P(("expert", "dp"), None),
            P(("expert", "dp"), None),
            P(("expert", "dp"), None),
            P(),
            P("expert", None, None),
            P("expert", None, None),
            P("expert", None, None),
        ),
        out_specs=(
            P(("expert", "dp"), None),
            P(("expert", "dp"), None),
            P("expert", "dp", None),
            P("expert", "dp", None),
            P("expert", None, "dp"),
        ),
        check_vma=False,
    )
```

time: 275 us -> 259 us (0.942)
  the two profiles are of different devices: /device:TPU:1 before, /device:TPU:97 now
where the time goes in v2:
time: 259 us
  Pallas kernels  245 us (95%)
  local copies, waits for them, and re-layouts  13.3 us (5%)
    pallas_call x1, Pallas kernels, shards(): pl.pallas_call(functools.partial(layer_kernel, expert_count, group_count,...  245 us
    unnamed x10, local copies, waits for them, and re-layouts  10.6 us

profile of v2, /device:TPU:97, one launch (start us, length us, event | category | flops | bytes accessed | tf_op | source)
XLA Modules:
  0.0 259.0 jit_solution(7126470889993095312)
XLA Ops:
  0.6 1.3 copy.15.rank
  2.0 1.4 copy.14.probs
  3.4 1.4 copy.13.routes
  4.8 245.0 %shard_map.119 = (bf16[128,2048]{1,0:T(8,128)(2,1)}, bf16[128,8]{1,0:T(8,128)(2,1)}, f32[1,512,768]{2,1,0:T(8,128)}, f32[1,512,768]{2,1,0:T(8,128)}, f32[1,768,512]{2,1,0:T(8,128)}) custom-call(bf16[128,2048]{1,0:T(8,128)(2,1)} %tokens.1, bf16[128,2048]{1,0:T(8,128)(2,1)} %cotangent.1, s32[128,8]{1,0:T(8,128)} %copy.13.routes, bf16[128,8]{1,0:T(8,128)(2,1)} %copy.14.probs, ...), custom_call_target="tpu_custom_call" | custom-call | flops 28991029248 | bytes 16777216 | tf_op jit(solution)/shard_map/pallas_call | solution.py:307
  249.8 1.4 copy.16
  251.2 1.9 copy.21
  253.1 0.0 copy-start.1
  253.1 2.8 %copy.22 = f32[1,512,768]{2,1,0:T(8,128)} copy(f32[1,512,768]{2,1,0:T(8,128)} %get-tuple-element.17) | data formatting | bytes 3145728
  255.9 0.0 copy-done.1
  255.9 0.0 copy-start
  255.9 1.1 copy.23
  257.0 0.8 copy-done
  257.8 1.1 copy.24
Async XLA Ops:
  253.1 2.8 %copy-start.1 = (f32[1,512,768]{2,1,0:T(8,128)S(1)}, f32[1,512,768]{2,1,0:T(8,128)}, u32[]{:S(2)}) copy-start(f32[1,512,768]{2,1,0:T(8,128)} %get-tuple-element.18) | copy-start | bytes 4718596
  255.9 2.0 copy-start

commit v3 on v2

v3 whole, which is shorter than its diff:
```python
import functools

import jax
import jax.numpy as jnp
from jax import lax
from jax.experimental import pallas as pl
from jax.experimental.pallas import tpu as pltpu
from jax.sharding import PartitionSpec as P

MESH = pl.DeviceIdType.MESH
NOTE = 128
FIRST = (((0,), (0,)), ((), ()))
LAST = (((1,), (1,)), ((), ()))
F32 = jnp.float32
BF16 = jnp.bfloat16


def dot(a, b, dims=(((1,), (0,)), ((), ()))):
    return lax.dot_general(a, b, dims, preferred_element_type=F32)


ORDER = (0, 1, 3, 2)
PAIRS = tuple(
    sorted(
        ((dz, dy) for dz in ORDER for dy in ORDER),
        key=lambda pair: (max(ORDER.index(pair[0]), ORDER.index(pair[1])), pair),
    )
)
SIDE = 4
CORES = 2
STEPS = (1, 3)


def layer_kernel(
    expert_count, group_count, slots, pick_count,
    tokens, cotangent, meta, gate_hbm, lift_hbm, down_hbm,
    tokens_grad, probs_grad, gate_change, lift_change, down_change,
    line_rows, line_meta, relayed, rows_in, place, x_turned, hidden_turned, deltas,
    back_out, back_in, sums_gl, sums_down,
    line_out_sem, line_in_sem, near_out_sem, near_in_sem, side_out_sem, side_in_sem,
    relay_out_sem, relay_in_sem, last_out_sem, last_in_sem, back_out_sem, back_in_sem, kernel_sem,
    gl_out_sem, gl_in_sem, down_out_sem, down_in_sem,
):
    me, group = lax.axis_index("expert"), lax.axis_index("dp")
    token_count, width = tokens.shape
    wide = width // 2
    inner = hidden_turned.shape[0]
    row_count = expert_count * slots
    quarter = width // group_count
    half_gl, half_down = quarter // 2, inner // 2
    chunk_pairs = len(PAIRS) // 4
    chunk_rows = chunk_pairs * CORES * slots
    up, down = (group + 1) % group_count, (group + group_count - 1) % group_count
    across = (group + 2) % group_count
    my_z, my_y, my_core = me // (SIDE * CORES), (me // CORES) % SIDE, me % CORES

    def device(dz, dy, core):
        z, y = (my_z + dz) % SIDE, (my_y + dy) % SIDE
        return (z * SIDE + y) * CORES + (my_core + core) % CORES

    def along(half, offset, core):
        return device(0, offset, core) if half == 0 else device(offset, 0, core)

    def pair_of(half, part, offset):
        offset %= SIDE
        return PAIRS.index((part, offset) if half == 0 else (offset, part))

    barrier = pltpu.get_barrier_semaphore()

    @pl.loop(1, expert_count)
    def _(step):
        pl.semaphore_signal(
            barrier, inc=1, device_id=((me + step) % expert_count, group), device_id_type=MESH
        )

    for neighbour in (up, down):
        pl.semaphore_signal(barrier, inc=1, device_id=(me, neighbour), device_id_type=MESH)

    def remote(source, target, send, receive, expert):
        return pltpu.make_async_remote_copy(
            src_ref=source,
            dst_ref=target,
            send_sem=send,
            recv_sem=receive,
            device_id=(expert, group),
            device_id_type=MESH,
        )

    def line_own(half, way, kind):
        columns = slice(half * wide, (half + 1) * wide)
        source = (tokens.at[:, columns], cotangent.at[:, columns], meta)[kind]
        slot = -STEPS[way] % SIDE - 1
        target = line_meta.at[half, slot] if kind == 2 else line_rows.at[half, slot, kind]
        return remote(
            source, target, line_out_sem.at[half, way, kind], line_in_sem.at[half, slot, kind],
            along(1 - half, STEPS[way], 0),
        )

    def line_on(half, kind):
        way = 1 if kind == 1 else 0
        slot = -STEPS[way] % SIDE - 1
        if kind == 2:
            source, target = line_meta.at[half, slot], line_meta.at[half, 1]
        else:
            source, target = line_rows.at[half, slot, kind], line_rows.at[half, 1, kind]
        return remote(
            source, target, line_out_sem.at[half, 2, kind], line_in_sem.at[half, 1, kind],
            along(1 - half, STEPS[way], 0),
        )

    def near(half, part, way, core, rows_out):
        offset = STEPS[way]
        return remote(
            rows_out.at[half, ORDER.index(part) % 2, offset, :, core],
            rows_in.at[half, pair_of(half, part, -offset), core],
            near_out_sem.at[half, part, way, core], near_in_sem.at[half, part, way, core],
            along(half, offset, core),
        )

    def beside(half, part, rows_out):
        return remote(
            rows_out.at[half, ORDER.index(part) % 2, 0, :, 1],
            rows_in.at[half, pair_of(half, part, 0), 1],
            side_out_sem.at[half, part], side_in_sem.at[half, part],
            along(half, 0, 1),
        )

    def relay(half, part, way, rows_out):
        return remote(
            rows_out.at[half, ORDER.index(part) % 2, 2, way],
            relayed.at[half, way, part],
            relay_out_sem.at[half, part, way], relay_in_sem.at[half, part, way],
            along(half, STEPS[way], 0),
        )

    def last(half, part, way, core):
        return remote(
            relayed.at[half, way, part, core],
            rows_in.at[half, pair_of(half, part, 2), core, way],
            last_out_sem.at[half, part, way, core], last_in_sem.at[half, part, way, core],
            along(half, STEPS[way], core),
        )

    def sends_of(half, part, rows_out):
        return (
            [beside(half, part, rows_out)]
            + [relay(half, part, way, rows_out) for way in range(2)]
            + [near(half, part, way, core, rows_out) for way in range(2) for core in range(CORES)]
        )

    below = jnp.where(
        lax.broadcasted_iota(jnp.int32, (token_count, token_count), 0)
        > lax.broadcasted_iota(jnp.int32, (token_count, token_count), 1),
        1.0,
        0.0,
    ).astype(BF16)
    shift = slots.bit_length() - 1

    def tables(facts, experts):
        lanes = len(experts) * slots
        lane = lax.broadcasted_iota(jnp.int32, (1, lanes), 1)
        block = lax.shift_right_logical(lane, shift)
        slot = lax.bitwise_and(lane, slots - 1).astype(F32)
        named = jnp.zeros((1, lanes), jnp.int32)
        for number, expert in enumerate(experts):
            named = jnp.where(block == number, expert, named)
        named = named.astype(F32)
        facts = facts.astype(F32)
        limit = jnp.zeros((token_count, lanes), F32)
        weight = jnp.zeros((token_count, lanes), F32)
        for pick in range(pick_count):
            hit = facts[:, pick : pick + 1] == named
            weight = jnp.where(hit, facts[:, pick_count + pick : pick_count + pick + 1], weight)
            first = 2 * pick_count + pick
            limit = jnp.where(hit, facts[:, first : first + 1], limit)
        order = dot(below, jnp.where(limit > 0.0, 1.0, 0.0).astype(BF16))
        kept = (order == slot) & (order < limit)
        return (
            jnp.where(kept, 1.0, 0.0).astype(BF16),
            jnp.where(kept, weight, 0.0).astype(BF16),
        )

    def first_part(rows_out, gate, lift, down_kernel):
        loads = [
            pltpu.make_async_copy(source, target, kernel_sem.at[i])
            for i, (source, target) in enumerate(
                ((gate_hbm, gate), (lift_hbm, lift), (down_hbm, down_kernel))
            )
        ]
        for load in loads:
            load.start()
        pl.semaphore_wait(barrier, expert_count + 1)
        for kind in (2, 0, 1):
            for way in range(2):
                for half in range(2):
                    line_own(half, way, kind).start()

        line_experts = [
            [along(half, offset, core) for offset in range(SIDE) for core in range(CORES)]
            for half in range(2)
        ]

        def send_part(part):
            for half in range(2):
                number = ORDER.index(part)
                if part == 0:
                    columns = slice(half * wide, (half + 1) * wide)
                    sources = (tokens[:, columns], cotangent[:, columns])
                    facts = meta[...]
                else:
                    sources = (line_rows[half, part - 1, 0], line_rows[half, part - 1, 1])
                    facts = line_meta[half, part - 1]
                if number >= 2:
                    for copy in sends_of(half, ORDER[number - 2], rows_out):
                        copy.wait_send()
                for kind, table in enumerate(tables(facts, line_experts[half])):
                    chosen = dot(table, sources[kind], FIRST).astype(BF16)
                    chosen = chosen.reshape(SIDE, CORES, slots, wide)
                    rows_out[half, number % 2, :, kind] = chosen
                    rows_in[half, pair_of(half, part, 0), 0, kind] = chosen[0, 0]
                for copy in sends_of(half, part, rows_out):
                    copy.start()

        def pass_last(part):
            for half in range(2):
                for way in range(2):
                    relay(half, part, way, rows_out).wait_recv()
                    for core in range(CORES):
                        last(half, part, way, core).start()

        send_part(0)
        for half in range(2):
            for kind in (2, 0, 1):
                line_own(half, 0, kind).wait_recv()
                line_own(half, 1, kind).wait_recv()
                line_on(half, kind).start()
        send_part(1)
        pass_last(0)
        send_part(3)
        pass_last(1)
        for half in range(2):
            for kind in range(3):
                line_on(half, kind).wait_recv()
        send_part(2)
        place[...] = tables(
            meta[...], [device(-dz, -dy, core) for dz, dy in PAIRS for core in range(CORES)]
        )[0]
        pass_last(3)
        for load in loads:
            load.wait()

        def await_rows(half, part, offset):
            if offset == 0:
                beside(half, part, rows_out).wait_recv()
            for core in range(CORES):
                if offset == 2:
                    for way in range(2):
                        last(half, part, way, core).wait_recv()
                elif offset:
                    near(half, part, 1 - STEPS.index(offset), core, rows_out).wait_recv()

        @pl.loop(0, len(PAIRS) // chunk_pairs)
        def _(part):
            blocks = pl.ds(part * chunk_pairs, chunk_pairs)
            rows = pl.ds(pl.multiple_of(part * chunk_rows, chunk_rows), chunk_rows)
            for number in range(len(PAIRS) // chunk_pairs):

                @pl.when(part == number)
                def _():
                    if number == 2:
                        pass_last(2)
                    for dz, dy in PAIRS[number * chunk_pairs : (number + 1) * chunk_pairs]:
                        await_rows(0, dz, dy)
                        await_rows(1, dy, dz)

            x, scaled = (
                jnp.concatenate(
                    [rows_in[half, blocks, :, kind].reshape(chunk_rows, wide) for half in range(2)],
                    axis=1,
                )
                for kind in range(2)
            )
            shape = (chunk_pairs * CORES, slots)
            blocks = pl.ds(part * chunk_pairs * CORES, chunk_pairs * CORES)
            x_turned[:, rows] = x.T
            gate_pre = dot(x, gate[...])
            lift_pre = dot(x, lift[...])
            sigmoid = jax.nn.sigmoid(gate_pre)
            activated = gate_pre * sigmoid
            hidden = (activated * lift_pre).astype(BF16)
            hidden_turned[:, rows] = hidden.T
            expert_out = dot(hidden, down_kernel[...])
            prob = jnp.sum(scaled.astype(F32) * expert_out, axis=1, keepdims=True)
            back_out[blocks, :, width:] = (
                jnp.broadcast_to(prob, (chunk_rows, NOTE)).astype(BF16).reshape(*shape, NOTE)
            )
            hidden_delta = dot(scaled, down_kernel[...], LAST)
            lift_delta = (hidden_delta * activated).astype(BF16)
            gate_delta = (
                hidden_delta * lift_pre * sigmoid * (1.0 + gate_pre * (1.0 - sigmoid))
            ).astype(BF16)
            deltas[rows, :inner] = gate_delta
            deltas[rows, inner:] = lift_delta
            route_delta = dot(gate_delta, gate[...], LAST) + dot(lift_delta, lift[...], LAST)
            back_out[blocks, :, :width] = route_delta.astype(BF16).reshape(*shape, width)

        for half in range(2):
            for kind in range(3):
                for way in range(2):
                    line_own(half, way, kind).wait_send()
                line_on(half, kind).wait_send()
            for part in ORDER:
                if part in ORDER[2:]:
                    for copy in sends_of(half, part, rows_out):
                        copy.wait_send()
                for way in range(2):
                    for core in range(CORES):
                        last(half, part, way, core).wait_send()

    kernel_shape = gate_hbm.shape
    pl.run_scoped(
        first_part,
        pltpu.VMEM((2, 2, SIDE, 2, CORES, slots, wide), BF16),
        pltpu.VMEM(kernel_shape, BF16),
        pltpu.VMEM(kernel_shape, BF16),
        pltpu.VMEM((inner, width), BF16),
    )

    def give_back(step):
        dz, dy = PAIRS[step // CORES]
        return remote(
            back_out.at[step], back_in.at[step], back_out_sem.at[step], back_in_sem.at[step],
            device(dz, dy, step % CORES),
        )

    def term_gl(part, half):
        rows = pl.ds(pl.multiple_of(part * quarter + half * half_gl, half_gl), half_gl)
        return dot(x_turned[rows, :], deltas[...])

    def term_down(part, half):
        fraction = wide // quarter
        columns = pl.ds(pl.multiple_of((part % fraction) * quarter, quarter), quarter)
        scaled = rows_in[part // fraction, :, :, 1, :, columns].reshape(row_count, quarter)
        return dot(hidden_turned[half * half_down : (half + 1) * half_down, :], scaled)

    def second_part(partial_gl, partial_down):
        plan = (
            (across, 0, down, None),
            (across, 1, up, None),
            (up, 0, up, None),
            (down, 1, down, None),
            (down, 0, down, 0),
            (up, 1, up, 1),
        )

        def pass_on(number, kind):
            source, sink, send, receive = (
                (partial_gl, sums_gl, gl_out_sem, gl_in_sem),
                (partial_down, sums_down, down_out_sem, down_in_sem),
            )[kind]
            return pltpu.make_async_remote_copy(
                src_ref=source.at[number],
                dst_ref=sink.at[number],
                send_sem=send.at[number],
                recv_sem=receive.at[number],
                device_id=(me, plan[number][2]),
                device_id_type=MESH,
            )

        for number, (part, half, _, taken) in enumerate(plan):
            term = term_gl(part, half)
            if taken is not None:
                pass_on(taken, 0).wait_recv()
                term = term + sums_gl[taken].astype(F32)
            partial_gl[number] = term.astype(BF16)
            pass_on(number, 0).start()
            term = term_down(part, half)
            if taken is not None:
                pass_on(taken, 1).wait_recv()
                term = term + sums_down[taken].astype(F32)
            partial_down[number] = term.astype(BF16)
            pass_on(number, 1).start()
            if number == 1:
                for step in range(1, expert_count):
                    give_back(step).start()

        for half in range(2):
            rows = slice(half * half_gl, (half + 1) * half_gl)
            term = term_gl(group, half)
            gate_change[0, rows, :] = term[:, :inner]
            lift_change[0, rows, :] = term[:, inner:]
            rows = slice(half * half_down, (half + 1) * half_down)
            down_change[0, rows, :] = term_down(group, half)

        back_in[0] = back_out[0]

        for step in range(1, expert_count):
            give_back(step).wait_recv()

        returned = back_in[:, :, :width].reshape(row_count, width)
        tokens_grad[...] = dot(place[...], returned).astype(BF16)
        notes = back_in[:, :, width:].reshape(row_count, NOTE)
        note_row = lax.broadcasted_iota(jnp.int32, (row_count, NOTE), 0)
        note_lane = lax.broadcasted_iota(jnp.int32, (row_count, NOTE), 1)
        note_step = lax.shift_right_logical(note_row, slots.bit_length() - 1)
        notes = jnp.where(note_step == note_lane, notes.astype(F32), 0.0).astype(BF16)
        by_step = dot(place[...], notes)
        note_lane = lax.broadcasted_iota(jnp.int32, (1, NOTE), 1)
        sender = jnp.full((1, NOTE), -1, jnp.int32)
        for number in range(expert_count):
            dz, dy = PAIRS[number // CORES]
            sender = jnp.where(note_lane == number, device(-dz, -dy, number % CORES), sender)
        sender = sender.astype(F32)
        facts = meta[...].astype(F32)
        pick_lane = lax.broadcasted_iota(jnp.int32, (token_count, pick_count), 1)
        total = jnp.zeros((token_count, pick_count), F32)
        for pick in range(pick_count):
            value = jnp.where(facts[:, pick : pick + 1] == sender, by_step, 0.0)
            value = jnp.sum(value, axis=1, keepdims=True)
            total = jnp.where(pick_lane == pick, value, total)
        probs_grad[...] = (total / facts[:, pick_count : 2 * pick_count]).astype(BF16)

        for half, numbers in ((0, (2, 4)), (1, (3, 5))):
            rows = slice(half * half_gl, (half + 1) * half_gl)
            for number in numbers:
                pass_on(number, 0).wait_recv()
                gate_change[0, rows, :] += sums_gl[number, :, :inner].astype(F32)
                lift_change[0, rows, :] += sums_gl[number, :, inner:].astype(F32)
            rows = slice(half * half_down, (half + 1) * half_down)
            for number in numbers:
                pass_on(number, 1).wait_recv()
                down_change[0, rows, :] += sums_down[number].astype(F32)

        for number in range(len(plan)):
            for kind in range(2):
                pass_on(number, kind).wait_send()

        for step in range(1, expert_count):
            give_back(step).wait_send()

    pl.run_scoped(
        second_part,
        pltpu.VMEM((6, half_gl, 2 * inner), BF16),
        pltpu.VMEM((6, half_down, quarter), BF16),
    )


def shards(
    tokens, cotangent, route_ids, gate_probs, expert_rank, gate_kernel, lift_kernel, down_kernel
):
    expert_count = lax.axis_size("expert")
    group_count = lax.axis_size("dp")
    token_count, pick_count = route_ids.shape
    width = tokens.shape[1]
    inner = gate_kernel.shape[2]
    slots = token_count * pick_count // expert_count
    row_count = expert_count * slots
    quarter = width // group_count
    hot = jnp.any(route_ids[:, :, None] == expert_rank[: expert_count // 2], axis=2)
    limit = jnp.where(hot, slots, slots // 2)
    meta = jnp.concatenate([route_ids.astype(BF16), gate_probs, limit.astype(BF16)], axis=1)
    meta = jnp.pad(meta, ((0, 0), (0, NOTE - meta.shape[1])))
    vmem, anywhere = pl.BlockSpec(memory_space=pltpu.VMEM), pl.BlockSpec(memory_space=pl.ANY)
    dma = pltpu.SemaphoreType.DMA
    return pl.pallas_call(
        functools.partial(layer_kernel, expert_count, group_count, slots, pick_count),
        out_shape=(
            jax.ShapeDtypeStruct(tokens.shape, BF16),
            jax.ShapeDtypeStruct(gate_probs.shape, BF16),
            jax.ShapeDtypeStruct((1, quarter, inner), F32),
            jax.ShapeDtypeStruct((1, quarter, inner), F32),
            jax.ShapeDtypeStruct((1, inner, quarter), F32),
        ),
        in_specs=[vmem] * 3 + [anywhere] * 3,
        out_specs=[vmem] * 5,
        scratch_shapes=[
            pltpu.VMEM((2, SIDE - 1, 2, token_count, width // 2), BF16),
            pltpu.VMEM((2, SIDE - 1, token_count, NOTE), BF16),
            pltpu.VMEM((2, 2, SIDE, CORES, slots, width // 2), BF16),
            pltpu.VMEM((2, len(PAIRS), CORES, 2, slots, width // 2), BF16),
            pltpu.VMEM((token_count, row_count), BF16),
            pltpu.VMEM((width, row_count), BF16),
            pltpu.VMEM((inner, row_count), BF16),
            pltpu.VMEM((row_count, 2 * inner), BF16),
            pltpu.VMEM((expert_count, slots, width + NOTE), BF16),
            pltpu.VMEM((expert_count, slots, width + NOTE), BF16),
            pltpu.VMEM((6, quarter // 2, 2 * inner), BF16),
            pltpu.VMEM((6, inner // 2, quarter), BF16),
            dma((2, 3, 3)),
            dma((2, 3, 3)),
            dma((2, SIDE, 2, CORES)),
            dma((2, SIDE, 2, CORES)),
            dma((2, SIDE)),
            dma((2, SIDE)),
            dma((2, SIDE, 2)),
            dma((2, SIDE, 2)),
            dma((2, SIDE, 2, CORES)),
            dma((2, SIDE, 2, CORES)),
            dma((expert_count,)),
            dma((expert_count,)),
            dma((3,)),
            dma((6,)),
            dma((6,)),
            dma((6,)),
            dma((6,)),
        ],
        compiler_params=pltpu.CompilerParams(
            collective_id=0, has_side_effects=True, vmem_limit_bytes=64 * 1024 * 1024
        ),
        cost_estimate=pl.CostEstimate(
            flops=18 * row_count * width * inner,
            bytes_accessed=16 * 1024 * 1024,
            transcendentals=row_count * inner,
        ),
    )(tokens, cotangent, meta, gate_kernel[0], lift_kernel[0], down_kernel[0])


def solution(mesh):
    return jax.shard_map(
        shards,
        mesh=mesh,
        in_specs=(
            P(("expert", "dp"), None),
            P(("expert", "dp"), None),
            P(("expert", "dp"), None),
            P(("expert", "dp"), None),
            P(),
            P("expert", None, None),
            P("expert", None, None),
            P("expert", None, None),
        ),
        out_specs=(
            P(("expert", "dp"), None),
            P(("expert", "dp"), None),
            P("expert", "dp", None),
            P("expert", "dp", None),
            P("expert", None, "dp"),
        ),
        check_vma=False,
    )
```

time: 259 us -> 180 us (0.69)
  the two profiles are of different devices: /device:TPU:97 before, /device:TPU:1 now
where the time goes in v3:
time: 180 us
  Pallas kernels  167 us (93%)
  local copies, waits for them, and re-layouts  9.93 us (6%)
  other arithmetic  2.17 us (1%)
    pallas_call x1, Pallas kernels, shards(): pl.pallas_call(functools.partial(layer_kernel, expert_count, group_count,...  167 us
    unnamed x8, local copies, waits for them, and re-layouts  7.77 us

profile of v3, /device:TPU:1, one launch (start us, length us, event | category | flops | bytes accessed | tf_op | source)
XLA Modules:
  0.0 180.0 jit_solution(462082565940317089)
XLA Ops:
  0.6 0.8 compare_reduce_fusion
  1.4 0.7 convert_element_type.8
  2.1 0.7 pad_maximum_fusion
  2.8 0.1 copy.20
  2.9 0.6 pad.4.meta
  3.6 167.2 %shard_map.119 = (bf16[128,2048]{1,0:T(8,128)(2,1)}, bf16[128,8]{1,0:T(8,128)(2,1)}, f32[1,512,768]{2,1,0:T(8,128)}, f32[1,512,768]{2,1,0:T(8,128)}, f32[1,768,512]{2,1,0:T(8,128)}) custom-call(bf16[128,2048]{1,0:T(8,128)(2,1)} %tokens.1, bf16[128,2048]{1,0:T(8,128)(2,1)} %cotangent.1, bf16[128,128]{1,0:T(8,128)(2,1)} %pad.4.meta, ...), custom_call_target="tpu_custom_call" | custom-call | flops 28991029248 | bytes 16777216 | tf_op jit(solution)/shard_map/pallas_call | solution.py:465
  170.8 1.4 copy.21
  172.2 1.9 %copy.26 = bf16[128,2048]{1,0:T(8,128)(2,1)} copy(bf16[128,2048]{1,0:T(8,128)(2,1)} %get-tuple-element.25) | data formatting | bytes 1048576
  174.1 0.0 copy-start.1
  174.1 2.8 %copy.27 = f32[1,512,768]{2,1,0:T(8,128)} copy(f32[1,512,768]{2,1,0:T(8,128)} %get-tuple-element.27) | data formatting | bytes 3145728
  176.8 0.0 copy-done.1
  176.8 0.0 copy-start
  176.8 1.1 copy.28
  178.0 0.8 copy-done
  178.8 1.1 copy.29
  (1 shorter events, 0.0 us)
Async XLA Ops:
  174.1 2.8 %copy-start.1 = (f32[1,512,768]{2,1,0:T(8,128)S(1)}, f32[1,512,768]{2,1,0:T(8,128)}, u32[]{:S(2)}) copy-start(f32[1,512,768]{2,1,0:T(8,128)} %get-tuple-element.28) | copy-start | bytes 4718596
  176.8 2.0 %copy-start = (f32[1,768,512]{2,1,0:T(8,128)S(1)}, f32[1,768,512]{2,1,0:T(8,128)}, u32[]{:S(2)}) copy-start(f32[1,768,512]{2,1,0:T(8,128)} %get-tuple-element.29) | copy-start | bytes 4718596

commit v4 on v3

--- a/solution.py
+++ b/solution.py
@@ -23,7 +23,7 @@
 PAIRS = tuple(
     sorted(
         ((dz, dy) for dz in ORDER for dy in ORDER),
-        key=lambda pair: (max(ORDER.index(pair[0]), ORDER.index(pair[1])), pair),
+        key=lambda pair: sorted((ORDER.index(pair[0]), ORDER.index(pair[1])), reverse=True),
     )
 )
 SIDE = 4
@@ -33,21 +33,22 @@
 
 def layer_kernel(
     expert_count, group_count, slots, pick_count,
-    tokens, cotangent, meta, gate_hbm, lift_hbm, down_hbm,
+    tokens, cotangent, routes, probs, rank, gate_hbm, lift_hbm, down_hbm,
     tokens_grad, probs_grad, gate_change, lift_change, down_change,
-    line_rows, line_meta, relayed, rows_in, place, x_turned, hidden_turned, deltas,
+    meta, line_rows, line_meta, relayed, rows_in, place, hidden_rows, deltas,
     back_out, back_in, sums_gl, sums_down,
     line_out_sem, line_in_sem, near_out_sem, near_in_sem, side_out_sem, side_in_sem,
     relay_out_sem, relay_in_sem, last_out_sem, last_in_sem, back_out_sem, back_in_sem, kernel_sem,
-    gl_out_sem, gl_in_sem, down_out_sem, down_in_sem,
+    sums_out_sem, sums_in_sem,
 ):
     me, group = lax.axis_index("expert"), lax.axis_index("dp")
     token_count, width = tokens.shape
     wide = width // 2
-    inner = hidden_turned.shape[0]
+    inner = hidden_rows.shape[1]
     row_count = expert_count * slots
     quarter = width // group_count
     half_gl, half_down = quarter // 2, inner // 2
+    piece_gl = half_gl // 2
     chunk_pairs = len(PAIRS) // 4
     chunk_rows = chunk_pairs * CORES * slots
     up, down = (group + 1) % group_count, (group + group_count - 1) % group_count
@@ -75,6 +76,21 @@
 
     for neighbour in (up, down):
         pl.semaphore_signal(barrier, inc=1, device_id=(me, neighbour), device_id_type=MESH)
+
+    experts = routes[...]
+    hot = experts == rank[0]
+    for place_number in range(1, expert_count // 2):
+        hot = hot | (experts == rank[place_number])
+    facts = jnp.concatenate(
+        [
+            experts.astype(F32),
+            probs[...].astype(F32),
+            jnp.where(hot, float(slots), float(slots // 2)),
+            jnp.zeros((NOTE - 3 * pick_count, token_count), F32),
+        ],
+        axis=0,
+    )
+    meta[...] = facts.T.astype(BF16)
 
     def remote(source, target, send, receive, expert):
         return pltpu.make_async_remote_copy(
@@ -111,7 +127,7 @@
     def near(half, part, way, core, rows_out):
         offset = STEPS[way]
         return remote(
-            rows_out.at[half, ORDER.index(part) % 2, offset, :, core],
+            rows_out.at[half, part, offset, :, core],
             rows_in.at[half, pair_of(half, part, -offset), core],
             near_out_sem.at[half, part, way, core], near_in_sem.at[half, part, way, core],
             along(half, offset, core),
@@ -119,7 +135,7 @@
 
     def beside(half, part, rows_out):
         return remote(
-            rows_out.at[half, ORDER.index(part) % 2, 0, :, 1],
+            rows_out.at[half, part, 0, :, 1],
             rows_in.at[half, pair_of(half, part, 0), 1],
             side_out_sem.at[half, part], side_in_sem.at[half, part],
             along(half, 0, 1),
@@ -127,7 +143,7 @@
 
     def relay(half, part, way, rows_out):
         return remote(
-            rows_out.at[half, ORDER.index(part) % 2, 2, way],
+            rows_out.at[half, part, 2, way],
             relayed.at[half, way, part],
             relay_out_sem.at[half, part, way], relay_in_sem.at[half, part, way],
             along(half, STEPS[way], 0),
@@ -202,7 +218,6 @@
 
         def send_part(part):
             for half in range(2):
-                number = ORDER.index(part)
                 if part == 0:
                     columns = slice(half * wide, (half + 1) * wide)
                     sources = (tokens[:, columns], cotangent[:, columns])
@@ -210,13 +225,10 @@
                 else:
                     sources = (line_rows[half, part - 1, 0], line_rows[half, part - 1, 1])
                     facts = line_meta[half, part - 1]
-                if number >= 2:
-                    for copy in sends_of(half, ORDER[number - 2], rows_out):
-                        copy.wait_send()
                 for kind, table in enumerate(tables(facts, line_experts[half])):
                     chosen = dot(table, sources[kind], FIRST).astype(BF16)
                     chosen = chosen.reshape(SIDE, CORES, slots, wide)
-                    rows_out[half, number % 2, :, kind] = chosen
+                    rows_out[half, part, :, kind] = chosen
                     rows_in[half, pair_of(half, part, 0), 0, kind] = chosen[0, 0]
                 for copy in sends_of(half, part, rows_out):
                     copy.start()
@@ -235,9 +247,8 @@
                 line_own(half, 1, kind).wait_recv()
                 line_on(half, kind).start()
         send_part(1)
+        send_part(3)
         pass_last(0)
-        send_part(3)
-        pass_last(1)
         for half in range(2):
             for kind in range(3):
                 line_on(half, kind).wait_recv()
@@ -245,6 +256,7 @@
         place[...] = tables(
             meta[...], [device(-dz, -dy, core) for dz, dy in PAIRS for core in range(CORES)]
         )[0]
+        pass_last(1)
         pass_last(3)
         for load in loads:
             load.wait()
@@ -267,7 +279,7 @@
 
                 @pl.when(part == number)
                 def _():
-                    if number == 2:
+                    if number == 1:
                         pass_last(2)
                     for dz, dy in PAIRS[number * chunk_pairs : (number + 1) * chunk_pairs]:
                         await_rows(0, dz, dy)
@@ -282,13 +294,12 @@
             )
             shape = (chunk_pairs * CORES, slots)
             blocks = pl.ds(part * chunk_pairs * CORES, chunk_pairs * CORES)
-            x_turned[:, rows] = x.T
             gate_pre = dot(x, gate[...])
             lift_pre = dot(x, lift[...])
             sigmoid = jax.nn.sigmoid(gate_pre)
             activated = gate_pre * sigmoid
             hidden = (activated * lift_pre).astype(BF16)
-            hidden_turned[:, rows] = hidden.T
+            hidden_rows[rows, :] = hidden
             expert_out = dot(hidden, down_kernel[...])
             prob = jnp.sum(scaled.astype(F32) * expert_out, axis=1, keepdims=True)
             back_out[blocks, :, width:] = (
@@ -310,9 +321,8 @@
                     line_own(half, way, kind).wait_send()
                 line_on(half, kind).wait_send()
             for part in ORDER:
-                if part in ORDER[2:]:
-                    for copy in sends_of(half, part, rows_out):
-                        copy.wait_send()
+                for copy in sends_of(half, part, rows_out):
+                    copy.wait_send()
                 for way in range(2):
                     for core in range(CORES):
                         last(half, part, way, core).wait_send()
@@ -320,7 +330,7 @@
     kernel_shape = gate_hbm.shape
     pl.run_scoped(
         first_part,
-        pltpu.VMEM((2, 2, SIDE, 2, CORES, slots, wide), BF16),
+        pltpu.VMEM((2, SIDE, SIDE, 2, CORES, slots, wide), BF16),
         pltpu.VMEM(kernel_shape, BF16),
         pltpu.VMEM(kernel_shape, BF16),
         pltpu.VMEM((inner, width), BF16),
@@ -333,15 +343,18 @@
             device(dz, dy, step % CORES),
         )
 
-    def term_gl(part, half):
-        rows = pl.ds(pl.multiple_of(part * quarter + half * half_gl, half_gl), half_gl)
-        return dot(x_turned[rows, :], deltas[...])
-
-    def term_down(part, half):
-        fraction = wide // quarter
-        columns = pl.ds(pl.multiple_of((part % fraction) * quarter, quarter), quarter)
-        scaled = rows_in[part // fraction, :, :, 1, :, columns].reshape(row_count, quarter)
-        return dot(hidden_turned[half * half_down : (half + 1) * half_down, :], scaled)
+    fraction = wide // quarter
+
+    def term(part, half, piece):
+        first = (part % fraction) * quarter
+        if piece == 2:
+            columns = pl.ds(pl.multiple_of(first, quarter), quarter)
+            scaled = rows_in[part // fraction, :, :, 1, :, columns].reshape(row_count, quarter)
+            return dot(hidden_rows[:, half * half_down : (half + 1) * half_down], scaled, FIRST)
+        first += half * half_gl + piece * piece_gl
+        columns = pl.ds(pl.multiple_of(first, piece_gl), piece_gl)
+        x = rows_in[part // fraction, :, :, 0, :, columns].reshape(row_count, piece_gl)
+        return dot(x, deltas[...], FIRST)
 
     def second_part(partial_gl, partial_down):
         plan = (
@@ -353,44 +366,55 @@
             (up, 1, up, 1),
         )
 
-        def pass_on(number, kind):
-            source, sink, send, receive = (
-                (partial_gl, sums_gl, gl_out_sem, gl_in_sem),
-                (partial_down, sums_down, down_out_sem, down_in_sem),
-            )[kind]
+        def view(gl, in_down, number, piece):
+            if piece == 2:
+                return in_down.at[number]
+            return gl.at[number, piece * piece_gl : (piece + 1) * piece_gl]
+
+        def pass_on(number, piece):
             return pltpu.make_async_remote_copy(
-                src_ref=source.at[number],
-                dst_ref=sink.at[number],
-                send_sem=send.at[number],
-                recv_sem=receive.at[number],
+                src_ref=view(partial_gl, partial_down, number, piece),
+                dst_ref=view(sums_gl, sums_down, number, piece),
+                send_sem=sums_out_sem.at[number, piece],
+                recv_sem=sums_in_sem.at[number, piece],
                 device_id=(me, plan[number][2]),
                 device_id_type=MESH,
             )
 
-        for number, (part, half, _, taken) in enumerate(plan):
-            term = term_gl(part, half)
-            if taken is not None:
-                pass_on(taken, 0).wait_recv()
-                term = term + sums_gl[taken].astype(F32)
-            partial_gl[number] = term.astype(BF16)
-            pass_on(number, 0).start()
-            term = term_down(part, half)
-            if taken is not None:
-                pass_on(taken, 1).wait_recv()
-                term = term + sums_down[taken].astype(F32)
-            partial_down[number] = term.astype(BF16)
-            pass_on(number, 1).start()
-            if number == 1:
-                for step in range(1, expert_count):
-                    give_back(step).start()
-
-        for half in range(2):
-            rows = slice(half * half_gl, (half + 1) * half_gl)
-            term = term_gl(group, half)
-            gate_change[0, rows, :] = term[:, :inner]
-            lift_change[0, rows, :] = term[:, inner:]
-            rows = slice(half * half_down, (half + 1) * half_down)
-            down_change[0, rows, :] = term_down(group, half)
+        def send_sums(numbers):
+            for piece in range(3):
+                for number in numbers:
+                    part, half, _, taken = plan[number]
+                    value = term(part, half, piece)
+                    if taken is not None:
+                        pass_on(taken, piece).wait_recv()
+                        value = value + view(sums_gl, sums_down, taken, piece)[...].astype(F32)
+                    view(partial_gl, partial_down, number, piece)[...] = value.astype(BF16)
+                    pass_on(number, piece).start()
+
+        def keep(half, piece, value, more):
+            if piece == 2:
+                rows = slice(half * half_down, (half + 1) * half_down)
+                targets = ((down_change, value),)
+            else:
+                rows = slice(half * half_gl + piece * piece_gl, half * half_gl + (piece + 1) * piece_gl)
+                targets = ((gate_change, value[:, :inner]), (lift_change, value[:, inner:]))
+            for target, values in targets:
+                target[0, rows, :] = target[0, rows, :] + values if more else values
+
+        def take(number, half, piece):
+            pass_on(number, piece).wait_recv()
+            value = view(sums_gl, sums_down, number, piece)[...].astype(F32)
+            keep(half, piece, value, True)
+
+        send_sums((0, 1))
+        for step in range(1, expert_count):
+            give_back(step).start()
+        send_sums((2, 3))
+        for piece in range(3):
+            for half in range(2):
+                keep(half, piece, term(group, half, piece), False)
+        send_sums((4, 5))
 
         back_in[0] = back_out[0]
 
@@ -418,22 +442,16 @@
             value = jnp.where(facts[:, pick : pick + 1] == sender, by_step, 0.0)
             value = jnp.sum(value, axis=1, keepdims=True)
             total = jnp.where(pick_lane == pick, value, total)
-        probs_grad[...] = (total / facts[:, pick_count : 2 * pick_count]).astype(BF16)
-
-        for half, numbers in ((0, (2, 4)), (1, (3, 5))):
-            rows = slice(half * half_gl, (half + 1) * half_gl)
-            for number in numbers:
-                pass_on(number, 0).wait_recv()
-                gate_change[0, rows, :] += sums_gl[number, :, :inner].astype(F32)
-                lift_change[0, rows, :] += sums_gl[number, :, inner:].astype(F32)
-            rows = slice(half * half_down, (half + 1) * half_down)
-            for number in numbers:
-                pass_on(number, 1).wait_recv()
-                down_change[0, rows, :] += sums_down[number].astype(F32)
-
+        total = jnp.concatenate([total, jnp.zeros((token_count, NOTE - pick_count), F32)], axis=1)
+        probs_grad[...] = (total.T[:pick_count] / probs[...].astype(F32)).astype(BF16)
+
+        for numbers in ((2, 3), (4, 5)):
+            for piece in range(3):
+                for half, number in enumerate(numbers):
+                    take(number, half, piece)
         for number in range(len(plan)):
-            for kind in range(2):
-                pass_on(number, kind).wait_send()
+            for piece in range(3):
+                pass_on(number, piece).wait_send()
 
         for step in range(1, expert_count):
             give_back(step).wait_send()
@@ -456,31 +474,27 @@
     slots = token_count * pick_count // expert_count
     row_count = expert_count * slots
     quarter = width // group_count
-    hot = jnp.any(route_ids[:, :, None] == expert_rank[: expert_count // 2], axis=2)
-    limit = jnp.where(hot, slots, slots // 2)
-    meta = jnp.concatenate([route_ids.astype(BF16), gate_probs, limit.astype(BF16)], axis=1)
-    meta = jnp.pad(meta, ((0, 0), (0, NOTE - meta.shape[1])))
     vmem, anywhere = pl.BlockSpec(memory_space=pltpu.VMEM), pl.BlockSpec(memory_space=pl.ANY)
     dma = pltpu.SemaphoreType.DMA
-    return pl.pallas_call(
+    outputs = pl.pallas_call(
         functools.partial(layer_kernel, expert_count, group_count, slots, pick_count),
         out_shape=(
-            jax.ShapeDtypeStruct(tokens.shape, BF16),
-            jax.ShapeDtypeStruct(gate_probs.shape, BF16),
-            jax.ShapeDtypeStruct((1, quarter, inner), F32),
-            jax.ShapeDtypeStruct((1, quarter, inner), F32),
-            jax.ShapeDtypeStruct((1, inner, quarter), F32),
+            pltpu.VMEM(tokens.shape, BF16),
+            pltpu.VMEM((pick_count, token_count), BF16),
+            pltpu.VMEM((1, quarter, inner), F32),
+            pltpu.VMEM((1, quarter, inner), F32),
+            pltpu.VMEM((1, inner, quarter), F32),
         ),
-        in_specs=[vmem] * 3 + [anywhere] * 3,
+        in_specs=[vmem] * 4 + [pl.BlockSpec(memory_space=pltpu.SMEM)] + [anywhere] * 3,
         out_specs=[vmem] * 5,
         scratch_shapes=[
+            pltpu.VMEM((token_count, NOTE), BF16),
             pltpu.VMEM((2, SIDE - 1, 2, token_count, width // 2), BF16),
             pltpu.VMEM((2, SIDE - 1, token_count, NOTE), BF16),
             pltpu.VMEM((2, 2, SIDE, CORES, slots, width // 2), BF16),
             pltpu.VMEM((2, len(PAIRS), CORES, 2, slots, width // 2), BF16),
             pltpu.VMEM((token_count, row_count), BF16),
-            pltpu.VMEM((width, row_count), BF16),
-            pltpu.VMEM((inner, row_count), BF16),
+            pltpu.VMEM((row_count, inner), BF16),
             pltpu.VMEM((row_count, 2 * inner), BF16),
             pltpu.VMEM((expert_count, slots, width + NOTE), BF16),
             pltpu.VMEM((expert_count, slots, width + NOTE), BF16),
@@ -499,20 +513,22 @@
             dma((expert_count,)),
             dma((expert_count,)),
             dma((3,)),
-            dma((6,)),
-            dma((6,)),
-            dma((6,)),
-            dma((6,)),
+            dma((6, 3)),
+            dma((6, 3)),
         ],
         compiler_params=pltpu.CompilerParams(
-            collective_id=0, has_side_effects=True, vmem_limit_bytes=64 * 1024 * 1024
+            collective_id=0, has_side_effects=True, vmem_limit_bytes=58 * 1024 * 1024
         ),
         cost_estimate=pl.CostEstimate(
             flops=18 * row_count * width * inner,
             bytes_accessed=16 * 1024 * 1024,
             transcendentals=row_count * inner,
         ),
-    )(tokens, cotangent, meta, gate_kernel[0], lift_kernel[0], down_kernel[0])
+    )(
+        tokens, cotangent, route_ids.T, gate_probs.T, expert_rank,
+        gate_kernel[0], lift_kernel[0], down_kernel[0],
+    )
+    return (outputs[0], outputs[1].T, *outputs[2:])
 
 
 def solution(mesh):

time: 180 us -> 170 us (0.944)
  local copies, waits for them, and re-layouts: 9.93 us -> 4.8 us
  other arithmetic: 2.17 us -> 0 us
  Pallas kernels: 167 us -> 165 us
    unnamed x8 -> x5, local copies, waits for them, and re-layouts: 7.77 us -> 4.8 us
    pallas_call x1, Pallas kernels: 167 us -> 165 us  [shards(): pl.pallas_call(functools.partial(layer_kernel, expert_count, group_count,...]
where the time goes in v4:
time: 170 us
  Pallas kernels  165 us (97%)
  local copies, waits for them, and re-layouts  4.8 us (3%)
    pallas_call x1, Pallas kernels, shards(): pl.pallas_call(functools.partial(layer_kernel, expert_count, group_count,...  165 us
    unnamed x5, local copies, waits for them, and re-layouts  4.8 us

profile of v4, /device:TPU:1, one launch (start us, length us, event | category | flops | bytes accessed | tf_op | source)
XLA Modules:
  0.0 169.9 jit_solution(12888842671268487782)
XLA Ops:
  0.6 164.5 %shard_map.119 = (bf16[128,2048]{1,0:T(8,128)(2,1)S(1)}, bf16[8,128]{1,0:T(8,128)(2,1)S(1)}, f32[1,512,768]{2,1,0:T(8,128)S(1)}, f32[1,512,768]{2,1,0:T(8,128)S(1)}, f32[1,768,512]{2,1,0:T(8,128)S(1)}) custom-call(bf16[128,2048]{1,0:T(8,128)(2,1)} %tokens.1, bf16[128,2048]{1,0:T(8,128)(2,1)} %cotangent.1, s32[8,128]{1,0:T(8,128)} %bitcast.10, ...), custom_call_target="tpu_custom_call" | custom-call | flops 28991029248 | bytes 16777216 | tf_op jit(solution)/shard_map/pallas_call | solution.py:479
  165.1 0.8 copy.18
  165.9 0.6 copy.19
  166.5 1.1 copy.20
  167.7 1.1 copy.21
  168.8 1.1 copy.22

commit v5 on v4

--- a/solution.py
+++ b/solution.py
@@ -8,6 +8,7 @@
 from jax.sharding import PartitionSpec as P
 
 MESH = pl.DeviceIdType.MESH
+FACTS = 32
 NOTE = 128
 FIRST = (((0,), (0,)), ((), ()))
 LAST = (((1,), (1,)), ((), ()))
@@ -36,6 +37,7 @@
     tokens, cotangent, routes, probs, rank, gate_hbm, lift_hbm, down_hbm,
     tokens_grad, probs_grad, gate_change, lift_change, down_change,
     meta, line_rows, line_meta, relayed, rows_in, place, hidden_rows, deltas,
+    gate, lift, down_kernel,
     back_out, back_in, sums_gl, sums_down,
     line_out_sem, line_in_sem, near_out_sem, near_in_sem, side_out_sem, side_in_sem,
     relay_out_sem, relay_in_sem, last_out_sem, last_in_sem, back_out_sem, back_in_sem, kernel_sem,
@@ -51,6 +53,7 @@
     piece_gl = half_gl // 2
     chunk_pairs = len(PAIRS) // 4
     chunk_rows = chunk_pairs * CORES * slots
+    chunks = len(PAIRS) // chunk_pairs
     up, down = (group + 1) % group_count, (group + group_count - 1) % group_count
     across = (group + 2) % group_count
     my_z, my_y, my_core = me // (SIDE * CORES), (me // CORES) % SIDE, me % CORES
@@ -68,14 +71,11 @@
 
     barrier = pltpu.get_barrier_semaphore()
 
-    @pl.loop(1, expert_count)
-    def _(step):
-        pl.semaphore_signal(
-            barrier, inc=1, device_id=((me + step) % expert_count, group), device_id_type=MESH
-        )
-
-    for neighbour in (up, down):
-        pl.semaphore_signal(barrier, inc=1, device_id=(me, neighbour), device_id_type=MESH)
+    neighbours = [(along(half, offset, core), group)
+                  for half in range(2) for offset in STEPS for core in range(CORES)]
+    neighbours += [(device(0, 0, 1), group), (me, up), (me, down)]
+    for neighbour in neighbours:
+        pl.semaphore_signal(barrier, inc=1, device_id=neighbour, device_id_type=MESH)
 
     experts = routes[...]
     hot = experts == rank[0]
@@ -86,11 +86,11 @@
             experts.astype(F32),
             probs[...].astype(F32),
             jnp.where(hot, float(slots), float(slots // 2)),
-            jnp.zeros((NOTE - 3 * pick_count, token_count), F32),
+            jnp.zeros((FACTS - 3 * pick_count, token_count), F32),
         ],
         axis=0,
     )
-    meta[...] = facts.T.astype(BF16)
+    meta[...] = facts.astype(BF16)
 
     def remote(source, target, send, receive, expert):
         return pltpu.make_async_remote_copy(
@@ -157,12 +157,13 @@
             along(half, STEPS[way], core),
         )
 
-    def sends_of(half, part, rows_out):
-        return (
-            [beside(half, part, rows_out)]
-            + [relay(half, part, way, rows_out) for way in range(2)]
-            + [near(half, part, way, core, rows_out) for way in range(2) for core in range(CORES)]
-        )
+    def relays_of(half, part, rows_out):
+        return [relay(half, part, way, rows_out) for way in range(2)]
+
+    def direct_of(half, part, rows_out):
+        return [beside(half, part, rows_out)] + [
+            near(half, part, way, core, rows_out) for way in range(2) for core in range(CORES)
+        ]
 
     below = jnp.where(
         lax.broadcasted_iota(jnp.int32, (token_count, token_count), 0)
@@ -181,7 +182,7 @@
         for number, expert in enumerate(experts):
             named = jnp.where(block == number, expert, named)
         named = named.astype(F32)
-        facts = facts.astype(F32)
+        facts = facts.astype(F32).T
         limit = jnp.zeros((token_count, lanes), F32)
         weight = jnp.zeros((token_count, lanes), F32)
         for pick in range(pick_count):
@@ -196,7 +197,38 @@
             jnp.where(kept, weight, 0.0).astype(BF16),
         )
 
-    def first_part(rows_out, gate, lift, down_kernel):
+    def chunk_of(part, kind):
+        blocks = pl.ds(part * chunk_pairs, chunk_pairs)
+        halves = [rows_in[half, blocks, :, kind].reshape(chunk_rows, wide) for half in range(2)]
+        return jnp.concatenate(halves, axis=1)
+
+    def first_half(part):
+        rows = pl.ds(pl.multiple_of(part * chunk_rows, chunk_rows), chunk_rows)
+        x = chunk_of(part, 0)
+        gate_pre = dot(x, gate[...])
+        lift_pre = dot(x, lift[...])
+        sigmoid = jax.nn.sigmoid(gate_pre)
+        activated = gate_pre * sigmoid
+        hidden_rows[rows, :] = (activated * lift_pre).astype(BF16)
+        hidden_delta = dot(chunk_of(part, 1), down_kernel[...], LAST)
+        deltas[rows, :inner] = (
+            hidden_delta * lift_pre * sigmoid * (1.0 + gate_pre * (1.0 - sigmoid))
+        ).astype(BF16)
+        deltas[rows, inner:] = (hidden_delta * activated).astype(BF16)
+
+    def second_half(part):
+        rows = pl.ds(pl.multiple_of(part * chunk_rows, chunk_rows), chunk_rows)
+        blocks = pl.ds(part * chunk_pairs * CORES, chunk_pairs * CORES)
+        shape = (chunk_pairs * CORES, slots)
+        expert_out = dot(hidden_rows[rows, :], down_kernel[...])
+        prob = jnp.sum(chunk_of(part, 1).astype(F32) * expert_out, axis=1, keepdims=True)
+        prob = jnp.broadcast_to(prob, (chunk_rows, NOTE)).astype(BF16)
+        back_out[blocks, :, width:] = prob.reshape(*shape, NOTE)
+        route_delta = dot(deltas[rows, :inner], gate[...], LAST)
+        route_delta = route_delta + dot(deltas[rows, inner:], lift[...], LAST)
+        back_out[blocks, :, :width] = route_delta.astype(BF16).reshape(*shape, width)
+
+    def first_part(rows_out):
         loads = [
             pltpu.make_async_copy(source, target, kernel_sem.at[i])
             for i, (source, target) in enumerate(
@@ -205,7 +237,7 @@
         ]
         for load in loads:
             load.start()
-        pl.semaphore_wait(barrier, expert_count + 1)
+        pl.semaphore_wait(barrier, len(neighbours))
         for kind in (2, 0, 1):
             for way in range(2):
                 for half in range(2):
@@ -216,21 +248,24 @@
             for half in range(2)
         ]
 
-        def send_part(part):
+        def choose(part):
             for half in range(2):
                 if part == 0:
                     columns = slice(half * wide, (half + 1) * wide)
                     sources = (tokens[:, columns], cotangent[:, columns])
-                    facts = meta[...]
+                    known = meta[...]
                 else:
                     sources = (line_rows[half, part - 1, 0], line_rows[half, part - 1, 1])
-                    facts = line_meta[half, part - 1]
-                for kind, table in enumerate(tables(facts, line_experts[half])):
+                    known = line_meta[half, part - 1]
+                for kind, table in enumerate(tables(known, line_experts[half])):
                     chosen = dot(table, sources[kind], FIRST).astype(BF16)
                     chosen = chosen.reshape(SIDE, CORES, slots, wide)
                     rows_out[half, part, :, kind] = chosen
                     rows_in[half, pair_of(half, part, 0), 0, kind] = chosen[0, 0]
-                for copy in sends_of(half, part, rows_out):
+
+        def send(part, copies_of):
+            for half in range(2):
+                for copy in copies_of(half, part, rows_out):
                     copy.start()
 
         def pass_last(part):
@@ -240,24 +275,31 @@
                     for core in range(CORES):
                         last(half, part, way, core).start()
 
-        send_part(0)
+        choose(0)
         for half in range(2):
             for kind in (2, 0, 1):
                 line_own(half, 0, kind).wait_recv()
                 line_own(half, 1, kind).wait_recv()
                 line_on(half, kind).start()
-        send_part(1)
-        send_part(3)
+        send(0, relays_of)
+        send(0, direct_of)
+        choose(1)
+        send(1, relays_of)
+        send(1, direct_of)
+        choose(3)
+        send(3, relays_of)
         pass_last(0)
         for half in range(2):
             for kind in range(3):
                 line_on(half, kind).wait_recv()
-        send_part(2)
+        choose(2)
+        send(2, relays_of)
+        send(3, direct_of)
+        send(2, direct_of)
         place[...] = tables(
             meta[...], [device(-dz, -dy, core) for dz, dy in PAIRS for core in range(CORES)]
         )[0]
         pass_last(1)
-        pass_last(3)
         for load in loads:
             load.wait()
 
@@ -271,49 +313,24 @@
                 elif offset:
                     near(half, part, 1 - STEPS.index(offset), core, rows_out).wait_recv()
 
-        @pl.loop(0, len(PAIRS) // chunk_pairs)
+        @pl.loop(0, chunks)
         def _(part):
-            blocks = pl.ds(part * chunk_pairs, chunk_pairs)
-            rows = pl.ds(pl.multiple_of(part * chunk_rows, chunk_rows), chunk_rows)
-            for number in range(len(PAIRS) // chunk_pairs):
+            for number in range(chunks):
 
                 @pl.when(part == number)
                 def _():
                     if number == 1:
+                        pass_last(3)
                         pass_last(2)
                     for dz, dy in PAIRS[number * chunk_pairs : (number + 1) * chunk_pairs]:
                         await_rows(0, dz, dy)
                         await_rows(1, dy, dz)
 
-            x, scaled = (
-                jnp.concatenate(
-                    [rows_in[half, blocks, :, kind].reshape(chunk_rows, wide) for half in range(2)],
-                    axis=1,
-                )
-                for kind in range(2)
-            )
-            shape = (chunk_pairs * CORES, slots)
-            blocks = pl.ds(part * chunk_pairs * CORES, chunk_pairs * CORES)
-            gate_pre = dot(x, gate[...])
-            lift_pre = dot(x, lift[...])
-            sigmoid = jax.nn.sigmoid(gate_pre)
-            activated = gate_pre * sigmoid
-            hidden = (activated * lift_pre).astype(BF16)
-            hidden_rows[rows, :] = hidden
-            expert_out = dot(hidden, down_kernel[...])
-            prob = jnp.sum(scaled.astype(F32) * expert_out, axis=1, keepdims=True)
-            back_out[blocks, :, width:] = (
-                jnp.broadcast_to(prob, (chunk_rows, NOTE)).astype(BF16).reshape(*shape, NOTE)
-            )
-            hidden_delta = dot(scaled, down_kernel[...], LAST)
-            lift_delta = (hidden_delta * activated).astype(BF16)
-            gate_delta = (
-                hidden_delta * lift_pre * sigmoid * (1.0 + gate_pre * (1.0 - sigmoid))
-            ).astype(BF16)
-            deltas[rows, :inner] = gate_delta
-            deltas[rows, inner:] = lift_delta
-            route_delta = dot(gate_delta, gate[...], LAST) + dot(lift_delta, lift[...], LAST)
-            back_out[blocks, :, :width] = route_delta.astype(BF16).reshape(*shape, width)
+            first_half(part)
+
+            @pl.when(part < chunks - 1)
+            def _():
+                second_half(part)
 
         for half in range(2):
             for kind in range(3):
@@ -321,20 +338,13 @@
                     line_own(half, way, kind).wait_send()
                 line_on(half, kind).wait_send()
             for part in ORDER:
-                for copy in sends_of(half, part, rows_out):
+                for copy in relays_of(half, part, rows_out) + direct_of(half, part, rows_out):
                     copy.wait_send()
                 for way in range(2):
                     for core in range(CORES):
                         last(half, part, way, core).wait_send()
 
-    kernel_shape = gate_hbm.shape
-    pl.run_scoped(
-        first_part,
-        pltpu.VMEM((2, SIDE, SIDE, 2, CORES, slots, wide), BF16),
-        pltpu.VMEM(kernel_shape, BF16),
-        pltpu.VMEM(kernel_shape, BF16),
-        pltpu.VMEM((inner, width), BF16),
-    )
+    pl.run_scoped(first_part, pltpu.VMEM((2, SIDE, SIDE, 2, CORES, slots, wide), BF16))
 
     def give_back(step):
         dz, dy = PAIRS[step // CORES]
@@ -381,15 +391,17 @@
                 device_id_type=MESH,
             )
 
-        def send_sums(numbers):
+        def send_sums(numbers, before=(None, None)):
             for piece in range(3):
-                for number in numbers:
+                for number, earlier in zip(numbers, before):
                     part, half, _, taken = plan[number]
                     value = term(part, half, piece)
                     if taken is not None:
                         pass_on(taken, piece).wait_recv()
                         value = value + view(sums_gl, sums_down, taken, piece)[...].astype(F32)
                     view(partial_gl, partial_down, number, piece)[...] = value.astype(BF16)
+                    if earlier is not None:
+                        pass_on(earlier, piece).wait_send()
                     pass_on(number, piece).start()
 
         def keep(half, piece, value, more):
@@ -408,13 +420,14 @@
             keep(half, piece, value, True)
 
         send_sums((0, 1))
+        second_half(chunks - 1)
         for step in range(1, expert_count):
             give_back(step).start()
-        send_sums((2, 3))
+        send_sums((3, 2), (0, 1))
         for piece in range(3):
             for half in range(2):
                 keep(half, piece, term(group, half, piece), False)
-        send_sums((4, 5))
+        send_sums((4, 5), (3, 2))
 
         back_in[0] = back_out[0]
 
@@ -435,7 +448,7 @@
             dz, dy = PAIRS[number // CORES]
             sender = jnp.where(note_lane == number, device(-dz, -dy, number % CORES), sender)
         sender = sender.astype(F32)
-        facts = meta[...].astype(F32)
+        facts = meta[...].astype(F32).T
         pick_lane = lax.broadcasted_iota(jnp.int32, (token_count, pick_count), 1)
         total = jnp.zeros((token_count, pick_count), F32)
         for pick in range(pick_count):
@@ -449,7 +462,7 @@
             for piece in range(3):
                 for half, number in enumerate(numbers):
                     take(number, half, piece)
-        for number in range(len(plan)):
+        for number in (4, 5):
             for piece in range(3):
                 pass_on(number, piece).wait_send()
 
@@ -461,6 +474,17 @@
         pltpu.VMEM((6, half_gl, 2 * inner), BF16),
         pltpu.VMEM((6, half_down, quarter), BF16),
     )
+
+
+def finish_kernel(*refs):
+    count = (len(refs) - 1) // 2
+    copies = [
+        pltpu.make_async_copy(refs[i], refs[count + i], refs[-1].at[i]) for i in range(count)
+    ]
+    for copy in copies:
+        copy.start()
+    for copy in copies:
+        copy.wait()
 
 
 def shards(
@@ -488,14 +512,17 @@
         in_specs=[vmem] * 4 + [pl.BlockSpec(memory_space=pltpu.SMEM)] + [anywhere] * 3,
         out_specs=[vmem] * 5,
         scratch_shapes=[
-            pltpu.VMEM((token_count, NOTE), BF16),
+            pltpu.VMEM((FACTS, token_count), BF16),
             pltpu.VMEM((2, SIDE - 1, 2, token_count, width // 2), BF16),
-            pltpu.VMEM((2, SIDE - 1, token_count, NOTE), BF16),
+            pltpu.VMEM((2, SIDE - 1, FACTS, token_count), BF16),
             pltpu.VMEM((2, 2, SIDE, CORES, slots, width // 2), BF16),
             pltpu.VMEM((2, len(PAIRS), CORES, 2, slots, width // 2), BF16),
             pltpu.VMEM((token_count, row_count), BF16),
             pltpu.VMEM((row_count, inner), BF16),
             pltpu.VMEM((row_count, 2 * inner), BF16),
+            pltpu.VMEM((width, inner), BF16),
+            pltpu.VMEM((width, inner), BF16),
+            pltpu.VMEM((inner, width), BF16),
             pltpu.VMEM((expert_count, slots, width + NOTE), BF16),
             pltpu.VMEM((expert_count, slots, width + NOTE), BF16),
             pltpu.VMEM((6, quarter // 2, 2 * inner), BF16),
@@ -528,6 +555,13 @@
         tokens, cotangent, route_ids.T, gate_probs.T, expert_rank,
         gate_kernel[0], lift_kernel[0], down_kernel[0],
     )
+    outputs = pl.pallas_call(
+        finish_kernel,
+        out_shape=[jax.ShapeDtypeStruct(item.shape, item.dtype) for item in outputs],
+        in_specs=[vmem] * 5,
+        out_specs=[anywhere] * 5,
+        scratch_shapes=[dma((5,))],
+    )(*outputs)
     return (outputs[0], outputs[1].T, *outputs[2:])
 
 

time: 170 us -> 172 us (1.012)
    pallas_call x0 -> x1, Pallas kernels: none -> 4.91 us  [shards(): pl.pallas_call(finish_kernel, out_shape=[jax.ShapeDtypeStruct(item.shape,...]
    pallas_call x1, Pallas kernels: 165 us -> 161 us  [shards(): pl.pallas_call(functools.partial(layer_kernel, expert_count, group_count,...]
    unnamed x5 -> x10, local copies, waits for them, and re-layouts: 4.8 us -> 4.85 us
where the time goes in v5:
time: 172 us
  Pallas kernels  166 us (97%)
  local copies, waits for them, and re-layouts  4.85 us (3%)
    pallas_call x1, Pallas kernels, shards(): pl.pallas_call(functools.partial(layer_kernel, expert_count, group_count,...  161 us
    pallas_call x1, Pallas kernels, shards(): pl.pallas_call(finish_kernel, out_shape=[jax.ShapeDtypeStruct(item.shape,...  4.91 us
    unnamed x10, local copies, waits for them, and re-layouts  4.85 us

profile of v5, /device:TPU:1, one launch (start us, length us, event | category | flops | bytes accessed | tf_op | source)
XLA Modules:
  0.0 172.0 jit_solution(3004972006226484173)
XLA Ops:
  0.6 161.4 %shard_map.119 = (bf16[128,2048]{1,0:T(8,128)(2,1)S(1)}, bf16[8,128]{1,0:T(8,128)(2,1)S(1)}, f32[1,512,768]{2,1,0:T(8,128)S(1)}, f32[1,512,768]{2,1,0:T(8,128)S(1)}, f32[1,768,512]{2,1,0:T(8,128)S(1)}) custom-call(bf16[128,2048]{1,0:T(8,128)(2,1)} %tokens.1, bf16[128,2048]{1,0:T(8,128)(2,1)} %cotangent.1, s32[8,128]{1,0:T(8,128)} %bitcast.9, ...), custom_call_target="tpu_custom_call" | custom-call | flops 28991029248 | bytes 16777216 | tf_op jit(solution)/shard_map/pallas_call | solution.py:503
  162.0 0.0 copy-start
  162.1 1.1 copy-done
  163.2 0.0 copy-start.1
  163.2 1.2 copy-done.1
  164.4 0.0 copy-start.2
  164.4 1.2 copy-done.2
  165.5 0.0 copy-start.3
  165.5 0.8 copy-done.3
  166.3 0.0 copy-start.4
  166.3 0.6 copy-done.4
  166.9 4.9 %shard_map.120 = (bf16[128,2048]{1,0:T(8,128)(2,1)}, bf16[8,128]{1,0:T(8,128)(2,1)}, f32[1,512,768]{2,1,0:T(8,128)}, f32[1,512,768]{2,1,0:T(8,128)}, f32[1,768,512]{2,1,0:T(8,128)}) custom-call(bf16[128,2048]{1,0:T(8,128)(2,1)} %copy-done.3, bf16[8,128]{1,0:T(8,128)(2,1)} %copy-done.4, f32[1,512,768]{2,1,0:T(8,128)} %copy-done, f32[1,512,768]{2,1,0:T(8,128)} %copy-done.1, ...), custom_call_target="tpu_custom_call" | custom-call | tf_op jit(solution)/shard_map/pallas_call | solution.py:558
Async XLA Ops:
  162.0 1.2 copy-start
  163.2 1.2 copy-start.1
  164.4 1.2 copy-start.2
  165.5 0.8 copy-start.3
  166.3 0.6 copy-start.4

commit v6 on v5

--- a/solution.py
+++ b/solution.py
@@ -27,8 +27,20 @@
         key=lambda pair: sorted((ORDER.index(pair[0]), ORDER.index(pair[1])), reverse=True),
     )
 )
+CORES = 2
+BACK = (1,) + tuple(
+    PAIRS.index(pair) * CORES + core
+    for pairs in (
+        ((0, 1), (1, 0), (0, 3), (3, 0)),
+        ((1, 1), (1, 3), (3, 1)),
+        ((3, 3), (0, 2), (2, 0)),
+        ((2, 1), (1, 2), (2, 3), (3, 2)),
+        ((2, 2),),
+    )
+    for core in range(CORES)
+    for pair in pairs
+)
 SIDE = 4
-CORES = 2
 STEPS = (1, 3)
 
 
@@ -157,12 +169,19 @@
             along(half, STEPS[way], core),
         )
 
-    def relays_of(half, part, rows_out):
-        return [relay(half, part, way, rows_out) for way in range(2)]
-
-    def direct_of(half, part, rows_out):
-        return [beside(half, part, rows_out)] + [
-            near(half, part, way, core, rows_out) for way in range(2) for core in range(CORES)
+    def relays_of(part, rows_out):
+        return [relay(half, part, way, rows_out) for way in range(2) for half in range(2)]
+
+    def direct_of(part, rows_out):
+        return [beside(half, part, rows_out) for half in range(2)] + [
+            near(half, part, way, core, rows_out)
+            for core in range(CORES) for way in range(2) for half in range(2)
+        ]
+
+    def lasts_of(part):
+        return [
+            last(half, part, way, core)
+            for core in range(CORES) for way in range(2) for half in range(2)
         ]
 
     below = jnp.where(
@@ -264,16 +283,14 @@
                     rows_in[half, pair_of(half, part, 0), 0, kind] = chosen[0, 0]
 
         def send(part, copies_of):
-            for half in range(2):
-                for copy in copies_of(half, part, rows_out):
-                    copy.start()
+            for copy in copies_of(part, rows_out):
+                copy.start()
 
         def pass_last(part):
-            for half in range(2):
-                for way in range(2):
-                    relay(half, part, way, rows_out).wait_recv()
-                    for core in range(CORES):
-                        last(half, part, way, core).start()
+            for copy in relays_of(part, rows_out):
+                copy.wait_recv()
+            for copy in lasts_of(part):
+                copy.start()
 
         choose(0)
         for half in range(2):
@@ -328,7 +345,7 @@
 
             first_half(part)
 
-            @pl.when(part < chunks - 1)
+            @pl.when(part < chunks // 2)
             def _():
                 second_half(part)
 
@@ -337,12 +354,9 @@
                 for way in range(2):
                     line_own(half, way, kind).wait_send()
                 line_on(half, kind).wait_send()
-            for part in ORDER:
-                for copy in relays_of(half, part, rows_out) + direct_of(half, part, rows_out):
-                    copy.wait_send()
-                for way in range(2):
-                    for core in range(CORES):
-                        last(half, part, way, core).wait_send()
+        for part in ORDER:
+            for copy in relays_of(part, rows_out) + direct_of(part, rows_out) + lasts_of(part):
+                copy.wait_send()
 
     pl.run_scoped(first_part, pltpu.VMEM((2, SIDE, SIDE, 2, CORES, slots, wide), BF16))
 
@@ -419,9 +433,12 @@
             value = view(sums_gl, sums_down, number, piece)[...].astype(F32)
             keep(half, piece, value, True)
 
+        split = CORES * len(PAIRS) // 2 - 1
         send_sums((0, 1))
-        second_half(chunks - 1)
-        for step in range(1, expert_count):
+        for step in BACK[:split]:
+            give_back(step).start()
+        pl.loop(chunks // 2, chunks)(second_half)
+        for step in BACK[split:]:
             give_back(step).start()
         send_sums((3, 2), (0, 1))
         for piece in range(3):
@@ -474,17 +491,6 @@
         pltpu.VMEM((6, half_gl, 2 * inner), BF16),
         pltpu.VMEM((6, half_down, quarter), BF16),
     )
-
-
-def finish_kernel(*refs):
-    count = (len(refs) - 1) // 2
-    copies = [
-        pltpu.make_async_copy(refs[i], refs[count + i], refs[-1].at[i]) for i in range(count)
-    ]
-    for copy in copies:
-        copy.start()
-    for copy in copies:
-        copy.wait()
 
 
 def shards(
@@ -555,13 +561,6 @@
         tokens, cotangent, route_ids.T, gate_probs.T, expert_rank,
         gate_kernel[0], lift_kernel[0], down_kernel[0],
     )
-    outputs = pl.pallas_call(
-        finish_kernel,
-        out_shape=[jax.ShapeDtypeStruct(item.shape, item.dtype) for item in outputs],
-        in_specs=[vmem] * 5,
-        out_specs=[anywhere] * 5,
-        scratch_shapes=[dma((5,))],
-    )(*outputs)
     return (outputs[0], outputs[1].T, *outputs[2:])
 
 

time: 172 us -> 166 us (0.965)
  Pallas kernels: 166 us -> 160 us
    pallas_call x1 -> x0, Pallas kernels: 4.91 us -> none  [shards(): pl.pallas_call(finish_kernel, out_shape=[jax.ShapeDtypeStruct(item.shape,...]
    unnamed x10 -> x5, local copies, waits for them, and re-layouts: 4.85 us -> 4.8 us
where the time goes in v6:
time: 166 us
  Pallas kernels  160 us (96%)
  local copies, waits for them, and re-layouts  4.8 us (3%)
    pallas_call x1, Pallas kernels, shards(): pl.pallas_call(functools.partial(layer_kernel, expert_count, group_count,...  160 us
    unnamed x5, local copies, waits for them, and re-layouts  4.8 us

profile of v6, /device:TPU:1, one launch (start us, length us, event | category | flops | bytes accessed | tf_op | source)
XLA Modules:
  0.0 165.6 jit_solution(4778648987039802757)
XLA Ops:
  0.6 160.2 %shard_map.119 = (bf16[128,2048]{1,0:T(8,128)(2,1)S(1)}, bf16[8,128]{1,0:T(8,128)(2,1)S(1)}, f32[1,512,768]{2,1,0:T(8,128)S(1)}, f32[1,512,768]{2,1,0:T(8,128)S(1)}, f32[1,768,512]{2,1,0:T(8,128)S(1)}) custom-call(bf16[128,2048]{1,0:T(8,128)(2,1)} %tokens.1, bf16[128,2048]{1,0:T(8,128)(2,1)} %cotangent.1, s32[8,128]{1,0:T(8,128)} %bitcast.10, ...), custom_call_target="tpu_custom_call" | custom-call | flops 28991029248 | bytes 16777216 | tf_op jit(solution)/shard_map/pallas_call | solution.py:509
  160.8 0.8 copy.18
  161.6 0.6 copy.19
  162.2 1.1 copy.20
  163.3 1.1 copy.21
  164.5 1.1 copy.22

commit v7 on v6

--- a/solution.py
+++ b/solution.py
@@ -41,18 +41,18 @@
     for pair in pairs
 )
 SIDE = 4
-STEPS = (1, 3)
+STEPS = (1, 3, 2)
 
 
 def layer_kernel(
     expert_count, group_count, slots, pick_count,
-    tokens, cotangent, routes, probs, rank, gate_hbm, lift_hbm, down_hbm,
+    tokens_hbm, cotangent_hbm, routes, probs, rank, gate_hbm, lift_hbm, down_hbm,
     tokens_grad, probs_grad, gate_change, lift_change, down_change,
-    meta, line_rows, line_meta, relayed, rows_in, place, hidden_rows, deltas,
+    tokens, cotangent, meta, line_rows, line_meta, rows_in, place, hidden_rows, deltas,
     gate, lift, down_kernel,
     back_out, back_in, sums_gl, sums_down,
     line_out_sem, line_in_sem, near_out_sem, near_in_sem, side_out_sem, side_in_sem,
-    relay_out_sem, relay_in_sem, last_out_sem, last_in_sem, back_out_sem, back_in_sem, kernel_sem,
+    back_out_sem, back_in_sem, kernel_sem, first_sem,
     sums_out_sem, sums_in_sem,
 ):
     me, group = lax.axis_index("expert"), lax.axis_index("dp")
@@ -89,6 +89,15 @@
     for neighbour in neighbours:
         pl.semaphore_signal(barrier, inc=1, device_id=neighbour, device_id_type=MESH)
 
+    firsts = [
+        pltpu.make_async_copy(source, target, first_sem.at[i])
+        for i, (source, target) in enumerate(
+            ((tokens_hbm, tokens), (cotangent_hbm, cotangent))
+        )
+    ]
+    for load in firsts:
+        load.start()
+
     experts = routes[...]
     hot = experts == rank[0]
     for place_number in range(1, expert_count // 2):
@@ -153,35 +162,10 @@
             along(half, 0, 1),
         )
 
-    def relay(half, part, way, rows_out):
-        return remote(
-            rows_out.at[half, part, 2, way],
-            relayed.at[half, way, part],
-            relay_out_sem.at[half, part, way], relay_in_sem.at[half, part, way],
-            along(half, STEPS[way], 0),
-        )
-
-    def last(half, part, way, core):
-        return remote(
-            relayed.at[half, way, part, core],
-            rows_in.at[half, pair_of(half, part, 2), core, way],
-            last_out_sem.at[half, part, way, core], last_in_sem.at[half, part, way, core],
-            along(half, STEPS[way], core),
-        )
-
-    def relays_of(part, rows_out):
-        return [relay(half, part, way, rows_out) for way in range(2) for half in range(2)]
-
-    def direct_of(part, rows_out):
+    def sends_of(part, rows_out):
         return [beside(half, part, rows_out) for half in range(2)] + [
             near(half, part, way, core, rows_out)
-            for core in range(CORES) for way in range(2) for half in range(2)
-        ]
-
-    def lasts_of(part):
-        return [
-            last(half, part, way, core)
-            for core in range(CORES) for way in range(2) for half in range(2)
+            for way in (2, 0, 1) for core in range(CORES) for half in range(2)
         ]
 
     below = jnp.where(
@@ -248,6 +232,14 @@
         back_out[blocks, :, :width] = route_delta.astype(BF16).reshape(*shape, width)
 
     def first_part(rows_out):
+        for load in firsts:
+            load.wait()
+        pl.semaphore_wait(barrier, len(neighbours))
+        for kind in (2, 0, 1):
+            for way in range(2):
+                for half in range(2):
+                    line_own(half, way, kind).start()
+
         loads = [
             pltpu.make_async_copy(source, target, kernel_sem.at[i])
             for i, (source, target) in enumerate(
@@ -256,12 +248,6 @@
         ]
         for load in loads:
             load.start()
-        pl.semaphore_wait(barrier, len(neighbours))
-        for kind in (2, 0, 1):
-            for way in range(2):
-                for half in range(2):
-                    line_own(half, way, kind).start()
-
         line_experts = [
             [along(half, offset, core) for offset in range(SIDE) for core in range(CORES)]
             for half in range(2)
@@ -282,14 +268,8 @@
                     rows_out[half, part, :, kind] = chosen
                     rows_in[half, pair_of(half, part, 0), 0, kind] = chosen[0, 0]
 
-        def send(part, copies_of):
-            for copy in copies_of(part, rows_out):
-                copy.start()
-
-        def pass_last(part):
-            for copy in relays_of(part, rows_out):
-                copy.wait_recv()
-            for copy in lasts_of(part):
+        def send(part):
+            for copy in sends_of(part, rows_out):
                 copy.start()
 
         choose(0)
@@ -298,37 +278,38 @@
                 line_own(half, 0, kind).wait_recv()
                 line_own(half, 1, kind).wait_recv()
                 line_on(half, kind).start()
-        send(0, relays_of)
-        send(0, direct_of)
+        send(0)
         choose(1)
-        send(1, relays_of)
-        send(1, direct_of)
+        send(1)
         choose(3)
-        send(3, relays_of)
-        pass_last(0)
+        send(3)
         for half in range(2):
             for kind in range(3):
                 line_on(half, kind).wait_recv()
         choose(2)
-        send(2, relays_of)
-        send(3, direct_of)
-        send(2, direct_of)
+        send(2)
         place[...] = tables(
             meta[...], [device(-dz, -dy, core) for dz, dy in PAIRS for core in range(CORES)]
         )[0]
-        pass_last(1)
         for load in loads:
             load.wait()
 
         def await_rows(half, part, offset):
             if offset == 0:
                 beside(half, part, rows_out).wait_recv()
-            for core in range(CORES):
-                if offset == 2:
+            else:
+                for core in range(CORES):
+                    near(half, part, STEPS.index(-offset % SIDE), core, rows_out).wait_recv()
+
+        def finish_sends():
+            for half in range(2):
+                for kind in range(3):
                     for way in range(2):
-                        last(half, part, way, core).wait_recv()
-                elif offset:
-                    near(half, part, 1 - STEPS.index(offset), core, rows_out).wait_recv()
+                        line_own(half, way, kind).wait_send()
+                    line_on(half, kind).wait_send()
+            for part in ORDER:
+                for copy in sends_of(part, rows_out):
+                    copy.wait_send()
 
         @pl.loop(0, chunks)
         def _(part):
@@ -336,9 +317,8 @@
 
                 @pl.when(part == number)
                 def _():
-                    if number == 1:
-                        pass_last(3)
-                        pass_last(2)
+                    if number == chunks - 1:
+                        finish_sends()
                     for dz, dy in PAIRS[number * chunk_pairs : (number + 1) * chunk_pairs]:
                         await_rows(0, dz, dy)
                         await_rows(1, dy, dz)
@@ -348,15 +328,6 @@
             @pl.when(part < chunks // 2)
             def _():
                 second_half(part)
-
-        for half in range(2):
-            for kind in range(3):
-                for way in range(2):
-                    line_own(half, way, kind).wait_send()
-                line_on(half, kind).wait_send()
-        for part in ORDER:
-            for copy in relays_of(part, rows_out) + direct_of(part, rows_out) + lasts_of(part):
-                copy.wait_send()
 
     pl.run_scoped(first_part, pltpu.VMEM((2, SIDE, SIDE, 2, CORES, slots, wide), BF16))
 
@@ -475,6 +446,8 @@
         total = jnp.concatenate([total, jnp.zeros((token_count, NOTE - pick_count), F32)], axis=1)
         probs_grad[...] = (total.T[:pick_count] / probs[...].astype(F32)).astype(BF16)
 
+        for step in range(1, expert_count):
+            give_back(step).wait_send()
         for numbers in ((2, 3), (4, 5)):
             for piece in range(3):
                 for half, number in enumerate(numbers):
@@ -482,9 +455,6 @@
         for number in (4, 5):
             for piece in range(3):
                 pass_on(number, piece).wait_send()
-
-        for step in range(1, expert_count):
-            give_back(step).wait_send()
 
     pl.run_scoped(
         second_part,
@@ -515,13 +485,14 @@
             pltpu.VMEM((1, quarter, inner), F32),
             pltpu.VMEM((1, inner, quarter), F32),
         ),
-        in_specs=[vmem] * 4 + [pl.BlockSpec(memory_space=pltpu.SMEM)] + [anywhere] * 3,
+        in_specs=[anywhere] * 2 + [vmem] * 2 + [pl.BlockSpec(memory_space=pltpu.SMEM)] + [anywhere] * 3,
         out_specs=[vmem] * 5,
         scratch_shapes=[
+            pltpu.VMEM(tokens.shape, BF16),
+            pltpu.VMEM(tokens.shape, BF16),
             pltpu.VMEM((FACTS, token_count), BF16),
             pltpu.VMEM((2, SIDE - 1, 2, token_count, width // 2), BF16),
             pltpu.VMEM((2, SIDE - 1, FACTS, token_count), BF16),
-            pltpu.VMEM((2, 2, SIDE, CORES, slots, width // 2), BF16),
             pltpu.VMEM((2, len(PAIRS), CORES, 2, slots, width // 2), BF16),
             pltpu.VMEM((token_count, row_count), BF16),
             pltpu.VMEM((row_count, inner), BF16),
@@ -535,17 +506,14 @@
             pltpu.VMEM((6, inner // 2, quarter), BF16),
             dma((2, 3, 3)),
             dma((2, 3, 3)),
-            dma((2, SIDE, 2, CORES)),
-            dma((2, SIDE, 2, CORES)),
+            dma((2, SIDE, 3, CORES)),
+            dma((2, SIDE, 3, CORES)),
             dma((2, SIDE)),
             dma((2, SIDE)),
-            dma((2, SIDE, 2)),
-            dma((2, SIDE, 2)),
-            dma((2, SIDE, 2, CORES)),
-            dma((2, SIDE, 2, CORES)),
             dma((expert_count,)),
             dma((expert_count,)),
             dma((3,)),
+            dma((2,)),
             dma((6, 3)),
             dma((6, 3)),
         ],

time: 166 us -> 167 us (level)
  no operation moved by 1% of the time
where the time goes in v7:
time: 167 us
  Pallas kernels  161 us (96%)
  local copies, waits for them, and re-layouts  4.8 us (3%)
    pallas_call x1, Pallas kernels, shards(): pl.pallas_call(functools.partial(layer_kernel, expert_count, group_count,...  161 us
    unnamed x5, local copies, waits for them, and re-layouts  4.8 us

profile of v7, /device:TPU:1, one launch (start us, length us, event | category | flops | bytes accessed | tf_op | source)
XLA Modules:
  0.0 166.6 jit_solution(8964974594444375720)
XLA Ops:
  0.6 161.1 %shard_map.119 = (bf16[128,2048]{1,0:T(8,128)(2,1)S(1)}, bf16[8,128]{1,0:T(8,128)(2,1)S(1)}, f32[1,512,768]{2,1,0:T(8,128)S(1)}, f32[1,512,768]{2,1,0:T(8,128)S(1)}, f32[1,768,512]{2,1,0:T(8,128)S(1)}) custom-call(bf16[128,2048]{1,0:T(8,128)(2,1)} %tokens_hbm.1, bf16[128,2048]{1,0:T(8,128)(2,1)} %cotangent_hbm.1, s32[8,128]{1,0:T(8,128)} %bitcast.10, ...), custom_call_target="tpu_custom_call" | custom-call | flops 28991029248 | bytes 16777216 | tf_op jit(solution)/shard_map/pallas_call | solution.py:479
  161.8 0.8 copy.18
  162.6 0.6 copy.19
  163.2 1.1 copy.20
  164.3 1.1 copy.21
  165.4 1.1 copy.22

commit v8 on v6

--- a/solution.py
+++ b/solution.py
@@ -40,19 +40,21 @@
     for core in range(CORES)
     for pair in pairs
 )
+PIECES = (2, 0, 1)
 SIDE = 4
 STEPS = (1, 3)
 
 
 def layer_kernel(
     expert_count, group_count, slots, pick_count,
-    tokens, cotangent, routes, probs, rank, gate_hbm, lift_hbm, down_hbm,
+    tokens_hbm, cotangent_hbm, routes, probs, rank, gate_hbm, lift_hbm, down_hbm,
     tokens_grad, probs_grad, gate_change, lift_change, down_change,
-    meta, line_rows, line_meta, relayed, rows_in, place, hidden_rows, deltas,
+    tokens, cotangent, meta, line_rows, line_meta, relayed, rows_in, place, hidden_rows, deltas,
     gate, lift, down_kernel,
-    back_out, back_in, sums_gl, sums_down,
+    back_out, back_in, sums_gl, sums_down, partial_down,
     line_out_sem, line_in_sem, near_out_sem, near_in_sem, side_out_sem, side_in_sem,
     relay_out_sem, relay_in_sem, last_out_sem, last_in_sem, back_out_sem, back_in_sem, kernel_sem,
+    first_sem,
     sums_out_sem, sums_in_sem,
 ):
     me, group = lax.axis_index("expert"), lax.axis_index("dp")
@@ -88,6 +90,15 @@
     neighbours += [(device(0, 0, 1), group), (me, up), (me, down)]
     for neighbour in neighbours:
         pl.semaphore_signal(barrier, inc=1, device_id=neighbour, device_id_type=MESH)
+
+    firsts = [
+        pltpu.make_async_copy(source, target, first_sem.at[i])
+        for i, (source, target) in enumerate(
+            ((tokens_hbm, tokens), (cotangent_hbm, cotangent))
+        )
+    ]
+    for load in firsts:
+        load.start()
 
     experts = routes[...]
     hot = experts == rank[0]
@@ -221,7 +232,7 @@
         halves = [rows_in[half, blocks, :, kind].reshape(chunk_rows, wide) for half in range(2)]
         return jnp.concatenate(halves, axis=1)
 
-    def first_half(part):
+    def first_half(part, between):
         rows = pl.ds(pl.multiple_of(part * chunk_rows, chunk_rows), chunk_rows)
         x = chunk_of(part, 0)
         gate_pre = dot(x, gate[...])
@@ -229,6 +240,7 @@
         sigmoid = jax.nn.sigmoid(gate_pre)
         activated = gate_pre * sigmoid
         hidden_rows[rows, :] = (activated * lift_pre).astype(BF16)
+        between()
         hidden_delta = dot(chunk_of(part, 1), down_kernel[...], LAST)
         deltas[rows, :inner] = (
             hidden_delta * lift_pre * sigmoid * (1.0 + gate_pre * (1.0 - sigmoid))
@@ -247,7 +259,65 @@
         route_delta = route_delta + dot(deltas[rows, inner:], lift[...], LAST)
         back_out[blocks, :, :width] = route_delta.astype(BF16).reshape(*shape, width)
 
+    fraction = wide // quarter
+
+    def term(part, half, piece):
+        first = (part % fraction) * quarter
+        if piece == 2:
+            columns = pl.ds(pl.multiple_of(first, quarter), quarter)
+            scaled = rows_in[part // fraction, :, :, 1, :, columns].reshape(row_count, quarter)
+            return dot(hidden_rows[:, half * half_down : (half + 1) * half_down], scaled, FIRST)
+        first += half * half_gl + piece * piece_gl
+        columns = pl.ds(pl.multiple_of(first, piece_gl), piece_gl)
+        x = rows_in[part // fraction, :, :, 0, :, columns].reshape(row_count, piece_gl)
+        return dot(x, deltas[...], FIRST)
+
+    plan = (
+        (across, 0, down, None),
+        (across, 1, up, None),
+        (up, 0, up, None),
+        (down, 1, down, None),
+        (down, 0, down, 0),
+        (up, 1, up, 1),
+    )
+
+    def view(gl, in_down, number, piece):
+        if piece == 2:
+            return in_down.at[number]
+        return gl.at[number, piece * piece_gl : (piece + 1) * piece_gl]
+
+    def pass_on(number, piece, partial_gl):
+        return pltpu.make_async_remote_copy(
+            src_ref=view(partial_gl, partial_down, number % 4, piece),
+            dst_ref=view(sums_gl, sums_down, number, piece),
+            send_sem=sums_out_sem.at[number, piece],
+            recv_sem=sums_in_sem.at[number, piece],
+            device_id=(me, plan[number][2]),
+            device_id_type=MESH,
+        )
+
+    def send_sums(partial_gl, numbers, pieces, before=(None, None)):
+        for piece in pieces:
+            for number, earlier in zip(numbers, before):
+                part, half, _, taken = plan[number]
+                value = term(part, half, piece)
+                if taken is not None:
+                    pass_on(taken, piece, partial_gl).wait_recv()
+                    value = value + view(sums_gl, sums_down, taken, piece)[...].astype(F32)
+                view(partial_gl, partial_down, number % 4, piece)[...] = value.astype(BF16)
+                if earlier is not None:
+                    pass_on(earlier, piece, partial_gl).wait_send()
+                pass_on(number, piece, partial_gl).start()
+
     def first_part(rows_out):
+        for load in firsts:
+            load.wait()
+        pl.semaphore_wait(barrier, len(neighbours))
+        for kind in (2, 0, 1):
+            for way in range(2):
+                for half in range(2):
+                    line_own(half, way, kind).start()
+
         loads = [
             pltpu.make_async_copy(source, target, kernel_sem.at[i])
             for i, (source, target) in enumerate(
@@ -256,12 +326,6 @@
         ]
         for load in loads:
             load.start()
-        pl.semaphore_wait(barrier, len(neighbours))
-        for kind in (2, 0, 1):
-            for way in range(2):
-                for half in range(2):
-                    line_own(half, way, kind).start()
-
         line_experts = [
             [along(half, offset, core) for offset in range(SIDE) for core in range(CORES)]
             for half in range(2)
@@ -330,12 +394,24 @@
                 elif offset:
                     near(half, part, 1 - STEPS.index(offset), core, rows_out).wait_recv()
 
+        def finish_sends():
+            for half in range(2):
+                for kind in range(3):
+                    for way in range(2):
+                        line_own(half, way, kind).wait_send()
+                    line_on(half, kind).wait_send()
+            for part in ORDER:
+                for copy in relays_of(part, rows_out) + direct_of(part, rows_out):
+                    copy.wait_send()
+
         @pl.loop(0, chunks)
         def _(part):
             for number in range(chunks):
 
                 @pl.when(part == number)
                 def _():
+                    if number == chunks - 1:
+                        finish_sends()
                     if number == 1:
                         pass_last(3)
                         pass_last(2)
@@ -343,20 +419,16 @@
                         await_rows(0, dz, dy)
                         await_rows(1, dy, dz)
 
-            first_half(part)
+            def between():
+                @pl.when(part == chunks - 1)
+                def _():
+                    send_sums(None, (0, 1), (2,))
+
+            first_half(part, between)
 
             @pl.when(part < chunks // 2)
             def _():
                 second_half(part)
-
-        for half in range(2):
-            for kind in range(3):
-                for way in range(2):
-                    line_own(half, way, kind).wait_send()
-                line_on(half, kind).wait_send()
-        for part in ORDER:
-            for copy in relays_of(part, rows_out) + direct_of(part, rows_out) + lasts_of(part):
-                copy.wait_send()
 
     pl.run_scoped(first_part, pltpu.VMEM((2, SIDE, SIDE, 2, CORES, slots, wide), BF16))
 
@@ -367,57 +439,7 @@
             device(dz, dy, step % CORES),
         )
 
-    fraction = wide // quarter
-
-    def term(part, half, piece):
-        first = (part % fraction) * quarter
-        if piece == 2:
-            columns = pl.ds(pl.multiple_of(first, quarter), quarter)
-            scaled = rows_in[part // fraction, :, :, 1, :, columns].reshape(row_count, quarter)
-            return dot(hidden_rows[:, half * half_down : (half + 1) * half_down], scaled, FIRST)
-        first += half * half_gl + piece * piece_gl
-        columns = pl.ds(pl.multiple_of(first, piece_gl), piece_gl)
-        x = rows_in[part // fraction, :, :, 0, :, columns].reshape(row_count, piece_gl)
-        return dot(x, deltas[...], FIRST)
-
-    def second_part(partial_gl, partial_down):
-        plan = (
-            (across, 0, down, None),
-            (across, 1, up, None),
-            (up, 0, up, None),
-            (down, 1, down, None),
-            (down, 0, down, 0),
-            (up, 1, up, 1),
-        )
-
-        def view(gl, in_down, number, piece):
-            if piece == 2:
-                return in_down.at[number]
-            return gl.at[number, piece * piece_gl : (piece + 1) * piece_gl]
-
-        def pass_on(number, piece):
-            return pltpu.make_async_remote_copy(
-                src_ref=view(partial_gl, partial_down, number, piece),
-                dst_ref=view(sums_gl, sums_down, number, piece),
-                send_sem=sums_out_sem.at[number, piece],
-                recv_sem=sums_in_sem.at[number, piece],
-                device_id=(me, plan[number][2]),
-                device_id_type=MESH,
-            )
-
-        def send_sums(numbers, before=(None, None)):
-            for piece in range(3):
-                for number, earlier in zip(numbers, before):
-                    part, half, _, taken = plan[number]
-                    value = term(part, half, piece)
-                    if taken is not None:
-                        pass_on(taken, piece).wait_recv()
-                        value = value + view(sums_gl, sums_down, taken, piece)[...].astype(F32)
-                    view(partial_gl, partial_down, number, piece)[...] = value.astype(BF16)
-                    if earlier is not None:
-                        pass_on(earlier, piece).wait_send()
-                    pass_on(number, piece).start()
-
+    def second_part(partial_gl):
         def keep(half, piece, value, more):
             if piece == 2:
                 rows = slice(half * half_down, (half + 1) * half_down)
@@ -429,22 +451,22 @@
                 target[0, rows, :] = target[0, rows, :] + values if more else values
 
         def take(number, half, piece):
-            pass_on(number, piece).wait_recv()
+            pass_on(number, piece, partial_gl).wait_recv()
             value = view(sums_gl, sums_down, number, piece)[...].astype(F32)
             keep(half, piece, value, True)
 
         split = CORES * len(PAIRS) // 2 - 1
-        send_sums((0, 1))
+        send_sums(partial_gl, (0, 1), (0, 1))
         for step in BACK[:split]:
             give_back(step).start()
         pl.loop(chunks // 2, chunks)(second_half)
         for step in BACK[split:]:
             give_back(step).start()
-        send_sums((3, 2), (0, 1))
+        send_sums(partial_gl, (3, 2), PIECES, (0, 1))
         for piece in range(3):
             for half in range(2):
                 keep(half, piece, term(group, half, piece), False)
-        send_sums((4, 5), (3, 2))
+        send_sums(partial_gl, (4, 5), PIECES, (3, 2))
 
         back_in[0] = back_out[0]
 
@@ -475,22 +497,21 @@
         total = jnp.concatenate([total, jnp.zeros((token_count, NOTE - pick_count), F32)], axis=1)
         probs_grad[...] = (total.T[:pick_count] / probs[...].astype(F32)).astype(BF16)
 
+        for step in range(1, expert_count):
+            give_back(step).wait_send()
         for numbers in ((2, 3), (4, 5)):
-            for piece in range(3):
+            for piece in PIECES:
                 for half, number in enumerate(numbers):
                     take(number, half, piece)
         for number in (4, 5):
             for piece in range(3):
-                pass_on(number, piece).wait_send()
-
-        for step in range(1, expert_count):
-            give_back(step).wait_send()
-
-    pl.run_scoped(
-        second_part,
-        pltpu.VMEM((6, half_gl, 2 * inner), BF16),
-        pltpu.VMEM((6, half_down, quarter), BF16),
-    )
+                pass_on(number, piece, partial_gl).wait_send()
+
+        for part in ORDER:
+            for copy in lasts_of(part):
+                copy.wait_send()
+
+    pl.run_scoped(second_part, pltpu.VMEM((4, half_gl, 2 * inner), BF16))
 
 
 def shards(
@@ -515,9 +536,11 @@
             pltpu.VMEM((1, quarter, inner), F32),
             pltpu.VMEM((1, inner, quarter), F32),
         ),
-        in_specs=[vmem] * 4 + [pl.BlockSpec(memory_space=pltpu.SMEM)] + [anywhere] * 3,
+        in_specs=[anywhere] * 2 + [vmem] * 2 + [pl.BlockSpec(memory_space=pltpu.SMEM)] + [anywhere] * 3,
         out_specs=[vmem] * 5,
         scratch_shapes=[
+            pltpu.VMEM(tokens.shape, BF16),
+            pltpu.VMEM(tokens.shape, BF16),
             pltpu.VMEM((FACTS, token_count), BF16),
             pltpu.VMEM((2, SIDE - 1, 2, token_count, width // 2), BF16),
             pltpu.VMEM((2, SIDE - 1, FACTS, token_count), BF16),
@@ -533,6 +556,7 @@
             pltpu.VMEM((expert_count, slots, width + NOTE), BF16),
             pltpu.VMEM((6, quarter // 2, 2 * inner), BF16),
             pltpu.VMEM((6, inner // 2, quarter), BF16),
+            pltpu.VMEM((4, inner // 2, quarter), BF16),
             dma((2, 3, 3)),
             dma((2, 3, 3)),
             dma((2, SIDE, 2, CORES)),
@@ -546,6 +570,7 @@
             dma((expert_count,)),
             dma((expert_count,)),
             dma((3,)),
+            dma((2,)),
             dma((6, 3)),
             dma((6, 3)),
         ],

time: 166 us -> 164 us (0.988)
  no operation moved by 1% of the time
where the time goes in v8:
time: 164 us
  Pallas kernels  159 us (97%)
  local copies, waits for them, and re-layouts  4.8 us (3%)
    pallas_call x1, Pallas kernels, shards(): pl.pallas_call(functools.partial(layer_kernel, expert_count, group_count,...  159 us
    unnamed x5, local copies, waits for them, and re-layouts  4.8 us

profile of v8, /device:TPU:1, one launch (start us, length us, event | category | flops | bytes accessed | tf_op | source)
XLA Modules:
  0.0 164.2 jit_solution(7138103479802624249)
XLA Ops:
  0.6 158.8 %shard_map.119 = (bf16[128,2048]{1,0:T(8,128)(2,1)S(1)}, bf16[8,128]{1,0:T(8,128)(2,1)S(1)}, f32[1,512,768]{2,1,0:T(8,128)S(1)}, f32[1,512,768]{2,1,0:T(8,128)S(1)}, f32[1,768,512]{2,1,0:T(8,128)S(1)}) custom-call(bf16[128,2048]{1,0:T(8,128)(2,1)} %tokens_hbm.1, bf16[128,2048]{1,0:T(8,128)(2,1)} %cotangent_hbm.1, s32[8,128]{1,0:T(8,128)} %bitcast.10, ...), custom_call_target="tpu_custom_call" | custom-call | flops 28991029248 | bytes 16777216 | tf_op jit(solution)/shard_map/pallas_call | solution.py:530
  159.4 0.8 copy.18
  160.2 0.6 copy.19
  160.8 1.1 copy.20
  161.9 1.1 copy.21
  163.1 1.1 copy.22
